TPU v7x, 256 devices: a whole 4x4x8 slice. The times are simulated.
256 devices in a mesh: dp: 8 (over x, z_lo), tensor: 32 (over y, z_hi, core).
Axes of the slice: x: 4, y: 4, z: 8 (z_hi: 4, z_lo: 2; z = z_hi * 2 + z_lo), core: 2. Of those that a mesh axis runs over, the one named last changes fastest.
Arguments:
- text: bfloat16 [2048, 8192], P('dp', 'tensor'), may hold values from -6 to 6
- grad_out: bfloat16 [2048, 8192], P('dp', 'tensor'), may hold values from -6 to 6
- vision: bfloat16 [2048, 7680], P('dp', 'tensor'), may hold values from -32 to 32
- gate: float32 [1], replicated, may hold values from 0.3 to 1.5
- w_query: bfloat16 [8192, 8192], P('dp', 'tensor'), may hold values from -0.0625 to 0.0625
- w_key: bfloat16 [7680, 1024], P('tensor', 'dp'), may hold values from -0.0625 to 0.0625
- w_value: bfloat16 [7680, 1024], P('tensor', 'dp'), may hold values from -0.0625 to 0.0625
- w_out: bfloat16 [8192, 8192], P('tensor', 'dp'), may hold values from -0.0625 to 0.0625
Outputs:
- update: bfloat16 [2048, 8192], P('dp', 'tensor')
- grad_text: bfloat16 [2048, 8192], P('dp', 'tensor')
- grad_vision: bfloat16 [2048, 7680], P('dp', 'tensor')
All inputs are finite; a program needn't handle non-finite values.
Results may differ from a plain program's by a relative error of at most 0.034.
Values may be sent and summed in bfloat16 or wider, within the bound.
A program may use at most 64 MiB of HBM per device.

v0:
```python
import jax
import jax.numpy as jnp
from jax import lax
from jax.sharding import PartitionSpec as P

KV_HEADS = 8
HEAD = 128


EPS = 1e-05


def rms_scale(tensor_in):
    return lax.rsqrt(jnp.mean(tensor_in * tensor_in, axis=-1, keepdims=True) + EPS)


def body(text, grad_out, vision, gate, w_query, w_key, w_value, w_out):
    texts, grads = (
        lax.all_gather(text, "tensor", axis=1, tiled=True),
        lax.all_gather(grad_out, "tensor", axis=1, tiled=True),
    )
    query_w, out_w, key_w, value_w = (
        lax.all_gather(w_query, "dp", axis=0, tiled=True),
        lax.all_gather(w_out, "dp", axis=1, tiled=True),
        lax.all_gather(w_key, "dp", axis=1, tiled=True),
        lax.all_gather(w_value, "dp", axis=1, tiled=True),
    )
    tensor_size = lax.axis_size("tensor")
    position = lax.axis_index("tensor")
    token_count = texts.shape[0]
    share = vision.shape[0] // tensor_size
    feature_count = vision.shape[1]
    per_head = tensor_size // KV_HEADS
    per_device = query_w.shape[1] // HEAD
    scale = HEAD ** (-0.5)
    gate_tanh = jnp.tanh(gate[0])
    joined_w = jnp.stack(
        (
            key_w.reshape(feature_count, KV_HEADS, HEAD),
            value_w.reshape(feature_count, KV_HEADS, HEAD),
        ),
        2,
    )
    joined_w = joined_w.reshape(feature_count, KV_HEADS * 2 * HEAD)
    projected = (
        lax.psum_scatter(
            jnp.dot(vision, joined_w, preferred_element_type=jnp.float32).astype(jnp.bfloat16),
            "tensor",
            scatter_dimension=0,
            tiled=True,
        )
        .astype(jnp.float32)
        .reshape(share, KV_HEADS, 2, HEAD)
    )
    keys = projected[:, :, 0]
    key_scale = rms_scale(keys)
    key_normed = (keys * key_scale).astype(jnp.bfloat16)
    values = projected[:, :, 1].astype(jnp.bfloat16)
    kv_share = jnp.concatenate((key_normed, values), 2)
    kv_index = position // per_head
    everything = lax.all_gather(kv_share, "tensor", axis=0, tiled=True)
    kv_head = lax.dynamic_index_in_dim(everything, kv_index, 1, keepdims=False)
    key_head = kv_head[:, :HEAD]
    value_head = kv_head[:, HEAD:]
    query = jnp.dot(texts, query_w, preferred_element_type=jnp.float32).reshape(
        token_count, per_device, HEAD
    )
    query_scale = rms_scale(query)
    query_normed = (query * query_scale).astype(jnp.bfloat16)
    scores = (
        jnp.einsum("thd,rd->thr", query_normed, key_head, preferred_element_type=jnp.float32)
        * scale
    )
    expo = jnp.exp(scores)
    probs = expo / jnp.sum(expo, axis=-1, keepdims=True)
    probs_low = probs.astype(jnp.bfloat16)
    attended = jnp.einsum("thr,rd->thd", probs_low, value_head, preferred_element_type=jnp.float32)
    attended = attended.astype(jnp.bfloat16).reshape(token_count, per_device * HEAD)
    out_part = jnp.dot(attended, out_w, preferred_element_type=jnp.float32)
    update = (
        gate_tanh
        * lax.psum_scatter(
            out_part.astype(jnp.bfloat16), "tensor", scatter_dimension=1, tiled=True
        ).astype(jnp.float32)
    ).astype(jnp.bfloat16)
    attend_grad = gate_tanh * jnp.einsum(
        "td,kd->tk", grads, out_w, preferred_element_type=jnp.float32
    )
    attend_grad = attend_grad.astype(jnp.bfloat16).reshape(token_count, per_device, HEAD)
    prob_grad = jnp.einsum(
        "thd,rd->thr", attend_grad, value_head, preferred_element_type=jnp.float32
    )
    delta = jnp.sum(probs * prob_grad, axis=-1, keepdims=True)
    score_grad = (probs * (prob_grad - delta) * scale).astype(jnp.bfloat16)
    normed_grad = jnp.einsum(
        "thr,rd->thd", score_grad, key_head, preferred_element_type=jnp.float32
    )
    query_grad = query_scale * normed_grad - query * query_scale**3 * jnp.mean(
        normed_grad * query, axis=-1, keepdims=True
    )
    query_grad = query_grad.astype(jnp.bfloat16).reshape(token_count, per_device * HEAD)
    input_part = jnp.einsum("tk,dk->td", query_grad, query_w, preferred_element_type=jnp.float32)
    grad_text = lax.psum_scatter(
        input_part.astype(jnp.bfloat16), "tensor", scatter_dimension=1, tiled=True
    )
    key_part = jnp.einsum(
        "thr,thd->rd", score_grad, query_normed, preferred_element_type=jnp.float32
    )
    value_part = jnp.einsum(
        "thr,thd->rd", probs_low, attend_grad, preferred_element_type=jnp.float32
    )
    kv_part = jnp.concatenate((key_part, value_part), 1).astype(jnp.bfloat16)
    selector = (jnp.arange(KV_HEADS, dtype=jnp.int32) == kv_index)[None, :, None]
    padded = jnp.where(selector, kv_part.astype(jnp.float32)[:, None, :], jnp.float32(0.0))
    kv_grads = lax.psum_scatter(
        padded.astype(jnp.bfloat16), "tensor", scatter_dimension=0, tiled=True
    ).astype(jnp.float32)
    key_side = kv_grads[:, :, :HEAD]
    value_grad = kv_grads[:, :, HEAD:]
    key_grad = key_scale * key_side - keys * key_scale**3 * jnp.mean(
        key_side * keys, axis=-1, keepdims=True
    )
    joined_grad = (
        jnp.stack((key_grad, value_grad), 2)
        .astype(jnp.bfloat16)
        .reshape(share, KV_HEADS * 2 * HEAD)
    )
    grad_vision = jnp.einsum(
        "rc,fc->rf",
        lax.all_gather(joined_grad, "tensor", axis=0, tiled=True),
        joined_w,
        preferred_element_type=jnp.float32,
    ).astype(jnp.bfloat16)
    return (update, grad_text, grad_vision)


def solution(mesh):
    return jax.shard_map(
        body,
        mesh=mesh,
        in_specs=(
            P("dp", "tensor"),
            P("dp", "tensor"),
            P("dp", "tensor"),
            P(),
            P("dp", "tensor"),
            P("tensor", "dp"),
            P("tensor", "dp"),
            P("tensor", "dp"),
        ),
        out_specs=(P("dp", "tensor"), P("dp", "tensor"), P("dp", "tensor")),
        check_vma=False,
    )
```

profile of v0, /device:TPU:1, one launch (start us, length us, event | category | flops | bytes accessed | tf_op | source)
XLA Modules:
  0.0 885.9 jit_solution(16365888618033213291)
XLA Ops:
  7.2 0.0 reduce-scatter.13.cloned.1.call-start
  7.2 23.6 %all_gather.26 = bf16[240,1024]{1,0:T(8,128)(2,1)S(1)} all-gather(bf16[240,128]{1,0:T(8,128)(2,1)} %param.13), channel_id=1, replica_groups=mesh['dp'=8,'tensor'=32] {'dp'}, dimensions={1}, use_global_device_ids=true | all-gather | bytes 552960 | tf_op jit(solution)/shard_map/all_gather | solution.py:25
  30.8 0.4 stack_reshape.8
  31.2 21.9 %all_gather.27 = bf16[240,1024]{1,0:T(8,128)(2,1)S(1)} all-gather(bf16[240,128]{1,0:T(8,128)(2,1)} %param.14), channel_id=1, replica_groups=mesh['dp'=8,'tensor'=32] {'dp'}, dimensions={1}, use_global_device_ids=true | all-gather | bytes 552960 | tf_op jit(solution)/shard_map/all_gather | solution.py:26
  53.1 0.4 stack_reshape.9
  53.5 2.2 pad_maximum_fusion
  55.7 0.8 reshape.89
  56.5 0.5 fusion.1
  57.0 1.4 copy.142
  58.4 0.0 reduce-scatter.13.cloned.1.call-update
  58.5 0.0 all-gather.11.cloned.1.call-start
  58.5 97.8 %reduce-scatter.13.cloned.1.call-done = bf16[8,2048]{1,0:T(8,128)(2,1)} async-done(((bf16[256,2048]{1,0:T(8,128)(2,1)}), bf16[8,2048]{1,0:T(8,128)(2,1)}) %reduce-scatter.13.cloned.1.call-update) | async-done | bytes 32784
  156.3 1.0 copy.143
  157.3 0.1 slice_convert_fusion
  157.4 0.2 copy.158
  157.6 0.1 multiply_reduce_fusion.3
  157.7 0.1 multiply_convert_fusion.4
  157.7 0.1 copy.146
  157.9 0.6 pad_maximum_fusion.1
  158.5 0.0 all-gather.9.cloned.1.call-start
  158.6 0.7 all-gather.9.cloned.1.call-update
  159.3 0.0 all-gather.7.cloned.1.call-start
  159.3 0.5 all-gather.7.cloned.1.call-update
  159.9 0.0 all-gather.13.cloned.1.call-start
  159.9 0.5 all-gather.13.cloned.1.call-update
  160.4 0.0 all-gather.15.cloned.1.call-start
  160.5 0.5 all-gather.15.cloned.1.call-update
  161.0 0.0 reduce-scatter.15.cloned.1.call-start
  161.8 50.0 %all-gather.11.cloned.1.call-done = bf16[256,8,256]{2,1,0:T(8,128)(2,1)} async-done(((bf16[8,8,256]{2,1,0:T(8,128)(2,1)}), bf16[256,8,256]{2,1,0:T(8,128)(2,1)}) %all-gather.11.cloned.1.call-update) | async-done | bytes 1048592 | tf_op jit(solution)/shard_map/all_gather | solution.py:61
  211.8 1.5 constant_dynamic-slice_fusion
  213.3 90.5 %all-gather.9.cloned.1.call-done = bf16[8192,256]{1,0:T(8,128)(2,1)} async-done(((bf16[1024,256]{1,0:T(8,128)(2,1)}), bf16[8192,256]{1,0:T(8,128)(2,1)}) %all-gather.9.cloned.1.call-update) | async-done | bytes 4194320 | tf_op jit(solution)/shard_map/all_gather | solution.py:23
  303.8 68.1 %all-gather.7.cloned.1.call-done = bf16[256,8192]{1,0:T(8,128)(2,1)} async-done(((bf16[256,256]{1,0:T(8,128)(2,1)}), bf16[256,8192]{1,0:T(8,128)(2,1)}) %all-gather.7.cloned.1.call-update) | async-done | bytes 4194320 | tf_op jit(solution)/shard_map/all_gather | solution.py:19
  371.9 5.2 multiply_reduce_fusion.2
  377.1 0.3 fusion.17
  377.4 0.2 fusion.2
  377.6 86.0 %all-gather.13.cloned.1.call-done = bf16[256,8192]{1,0:T(8,128)(2,1)} async-done(((bf16[256,1024]{1,0:T(8,128)(2,1)}), bf16[256,8192]{1,0:T(8,128)(2,1)}) %all-gather.13.cloned.1.call-update) | async-done | bytes 4194320 | tf_op jit(solution)/shard_map/all_gather | solution.py:24
  463.6 68.1 %all-gather.15.cloned.1.call-done = bf16[256,8192]{1,0:T(8,128)(2,1)} async-done(((bf16[256,256]{1,0:T(8,128)(2,1)}), bf16[256,8192]{1,0:T(8,128)(2,1)}) %all-gather.15.cloned.1.call-update) | async-done | bytes 4194320 | tf_op jit(solution)/shard_map/all_gather | solution.py:20
  531.7 4.8 fusion.7
  536.5 0.1 copy.156
  536.6 0.2 fusion.22
  536.8 0.3 fusion.9
  537.1 0.3 fusion.8
  537.4 0.1 copy.127
  537.5 0.2 fusion.11
  537.8 1.2 copy.157
  539.0 0.0 all-gather.17.cloned.1.call-start
  539.1 84.1 %reduce-scatter.15.cloned.1.call-done = bf16[8,2048]{1,0:T(8,128)(2,1)} async-done(((bf16[256,2048]{1,0:T(8,128)(2,1)}), bf16[8,2048]{1,0:T(8,128)(2,1)}) %reduce-scatter.15.cloned.1.call-update) | async-done | bytes 32784
  623.2 0.7 fusion.34
  624.0 0.1 fusion.25
  624.0 0.1 fusion.26
  624.2 0.6 convert_element_type.84
  624.8 0.0 all-gather.17.cloned.1.call-update
  624.9 0.0 reduce-scatter.9.cloned.1.call-start
  624.9 0.3 convolution_convert_fusion.3
  625.2 5.4 convolution_convert_fusion.1
  630.6 0.0 reduce-scatter.9.cloned.1.call-update
  630.6 0.0 reduce-scatter.11.cloned.1.call-start
  630.7 0.3 multiply_reduce_fusion.1
  631.1 5.5 convolution_convert_fusion
  636.6 41.7 %all-gather.17.cloned.1.call-done = bf16[256,2048]{1,0:T(8,128)(2,1)} async-done(((bf16[8,2048]{1,0:T(8,128)(2,1)}), bf16[256,2048]{1,0:T(8,128)(2,1)}) %all-gather.17.cloned.1.call-update) | async-done | bytes 1048592 | tf_op jit(solution)/shard_map/all_gather | solution.py:130
  678.3 2.4 convolution_convert_fusion.4
  680.7 96.5 %reduce-scatter.9.cloned.1.call-done = bf16[256,256]{1,0:T(8,128)(2,1)} async-done(((bf16[256,8192]{1,0:T(8,128)(2,1)}), bf16[256,256]{1,0:T(8,128)(2,1)}) %reduce-scatter.9.cloned.1.call-update) | async-done | bytes 131088 | tf_op jit(solution)/shard_map/reduce_scatter | solution.py:82
  777.2 1.6 multiply_convert_fusion
  778.8 100.3 %reduce-scatter.11.cloned.1.call-done = bf16[256,256]{1,0:T(8,128)(2,1)} async-done(((bf16[256,8192]{1,0:T(8,128)(2,1)}), bf16[256,256]{1,0:T(8,128)(2,1)}) %reduce-scatter.11.cloned.1.call-update) | async-done | bytes 131088 | tf_op jit(solution)/shard_map/reduce_scatter | solution.py:103
  (16 shorter events, 0.2 us)
Async XLA Ops:
  7.2 49.3 %copy-start = (bf16[256,240]{0,1:T(8,128)(2,1)S(1)}, bf16[256,240]{0,1:T(8,128)(2,1)}, u32[]{:S(2)}) copy-start(bf16[256,240]{0,1:T(8,128)(2,1)} %param.10) | copy-start | bytes 368644
  7.2 149.1 %reduce-scatter.13.cloned.1.call-start = ((), (), s32[]{:S(2)}) async-start(), calls=%async_computation.12 | async-start | bytes 1081344
  58.5 153.3 %all-gather.11.cloned.1.call-start = ((), (), s32[]{:S(2)}) async-start(), calls=%async_computation.6 | async-start | bytes 1081344 | tf_op jit(solution)/shard_map/all_gather | solution.py:61
  158.5 145.3 %all-gather.9.cloned.1.call-start = ((), (), s32[]{:S(2)}) async-start(), calls=%async_computation.5 | async-start | bytes 4718592 | tf_op jit(solution)/shard_map/all_gather | solution.py:23
  159.3 212.6 %all-gather.7.cloned.1.call-start = ((), (), s32[]{:S(2)}) async-start(), calls=%async_computation.4 | async-start | bytes 4325376 | tf_op jit(solution)/shard_map/all_gather | solution.py:19
  159.9 303.8 %all-gather.13.cloned.1.call-start = ((), (), s32[]{:S(2)}) async-start(), calls=%async_computation.7 | async-start | bytes 4718592 | tf_op jit(solution)/shard_map/all_gather | solution.py:24
  160.4 371.3 %all-gather.15.cloned.1.call-start = ((), (), s32[]{:S(2)}) async-start(), calls=%async_computation.9 | async-start | bytes 4325376 | tf_op jit(solution)/shard_map/all_gather | solution.py:20
  161.0 462.2 %reduce-scatter.15.cloned.1.call-start = ((), (), s32[]{:S(2)}) async-start(), calls=%async_computation.13 | async-start | bytes 1081344
  539.0 139.3 %all-gather.17.cloned.1.call-start = ((), (), s32[]{:S(2)}) async-start(), calls=%async_computation.11 | async-start | bytes 1081344 | tf_op jit(solution)/shard_map/all_gather | solution.py:130
  624.9 152.3 %reduce-scatter.9.cloned.1.call-start = ((), (), s32[]{:S(2)}) async-start(), calls=%async_computation.8 | async-start | bytes 4325376 | tf_op jit(solution)/shard_map/reduce_scatter | solution.py:82
  630.6 248.4 %reduce-scatter.11.cloned.1.call-start = ((), (), s32[]{:S(2)}) async-start(), calls=%async_computation.10 | async-start | bytes 4325376 | tf_op jit(solution)/shard_map/reduce_scatter | solution.py:103
Sparse Core Ops, SparseCore 0:
  58.6 97.6 reduce-scatter.12
  159.7 52.0 all-gather.10
  213.7 90.0 all-gather.8
  306.4 65.3 all-gather.6
  373.7 89.9 all-gather.12
  466.3 65.3 all-gather.14
  539.1 84.0 reduce-scatter.14
  626.3 51.9 all-gather.16
  682.3 94.8 reduce-scatter.8
  782.1 96.9 reduce-scatter.10
where the time goes:
time: 887 us; the launch traced here: 886 us
  waiting for transfers between devices  785 us (89%)
  blocking collectives  45.5 us (5%)
  matrix products  25.6 us (3%)
  between operations  15.1 us (2%)
    unnamed x12, waiting for transfers between devices  184 us
    reduce_scatter x1, waiting for transfers between devices, body(): lax.psum_scatter(input_part.astype(jnp.bfloat16), 'tensor', scatter_dimen...  100 us
    reduce_scatter x1, waiting for transfers between devices, body(): lax.psum_scatter(out_part.astype(jnp.bfloat16), 'tensor', scatter_dimensi...  96.5 us
    all_gather x1, waiting for transfers between devices, body(): lax.all_gather(w_query, 'dp', axis=0, tiled=True)  90.5 us
    all_gather x1, waiting for transfers between devices, body(): lax.all_gather(w_out, 'dp', axis=1, tiled=True)  86 us
    all_gather x1, waiting for transfers between devices, body(): lax.all_gather(text, 'tensor', axis=1, tiled=True)  68.1 us
    all_gather x1, waiting for transfers between devices, body(): lax.all_gather(grad_out, 'tensor', axis=1, tiled=True)  68.1 us
    all_gather x1, waiting for transfers between devices, body(): everything = lax.all_gather(kv_share, 'tensor', axis=0, tiled=True)  50 us
  transfers between devices with their start and end apart: 10, of which 10 were waited for; matrix products, arithmetic and copies ran while one was open for 3% of the time, Pallas kernels for 0%

commit v1 on v0

v1 whole, which is shorter than its diff:
```python
import jax
import jax.numpy as jnp
from jax import lax
from jax.experimental import pallas as pl
from jax.experimental.pallas import tpu as pltpu
from jax.sharding import PartitionSpec as P

HEAD = 128
EPS = 1e-05
MESH = pl.DeviceIdType.MESH
F32 = jnp.float32
BF16 = jnp.bfloat16
OFFSETS = (0, 3, 1, 2)
NT = (((1,), (1,)), ((), ()))
TN = (((0,), (0,)), ((), ()))


def dot(a, b, dims=(((1,), (0,)), ((), ()))):
    return lax.dot_general(a, b, dims, preferred_element_type=F32)


class Here:
    def __init__(self):
        d, t = lax.axis_index("dp"), lax.axis_index("tensor")
        self.x, self.zl = d // 2, d % 2
        self.y, self.zh, self.c = t // 8, (t // 2) % 4, t % 2
        self.z = 2 * self.zh + self.zl
        self.half = self.zh // 2

    def at(self, dx=0, dy=0, z=None, c=None):
        x = (self.x + dx) % 4 if dx else self.x
        y = (self.y + dy) % 4 if dy else self.y
        z = self.z if z is None else z
        c = self.c if c is None else c
        return (x * 2 + z % 2, y * 8 + (z // 2) * 2 + c)


def rcopy(src, dst, send, recv, device):
    return pltpu.make_async_remote_copy(
        src_ref=src, dst_ref=dst, send_sem=send, recv_sem=recv, device_id=device, device_id_type=MESH
    )


class Sends:
    def __init__(self):
        self.waits = []

    def start(self, *args):
        copy = rcopy(*args)
        copy.start()
        self.waits.append(copy.wait_send)

    def start_unless_self(self, me, z, src, dst, send, recv, device):
        @pl.when(z != me.z)
        def _():
            rcopy(src, dst, send, recv, device).start()

        @pl.when(z == me.z)
        def _():
            pltpu.make_async_copy(src, dst, recv).start()

        def finish():
            @pl.when(z != me.z)
            def _():
                rcopy(src, dst, send, recv, device).wait_send()

        self.waits.append(finish)

    def finish(self):
        for wait in self.waits:
            wait()


def arrived(dst, sem):
    pltpu.make_async_copy(dst, dst, sem).wait()


class RingGather:
    def __init__(self, me, sends, own, buf, cut, sems):
        self.me, self.sends, self.own, self.buf, self.cut = me, sends, own, buf, cut
        self.ss, self.rs = sems

    def start(self):
        me = self.me
        for way, dx in enumerate((1, -1)):
            self.sends.start(self.own, self.buf.at[me.x], self.ss.at[way], self.rs.at[way], me.at(dx=dx))

    def part(self, slot, way):
        rows = self.buf.shape[1]
        lo, n = ((0, self.cut), (self.cut, rows - self.cut))[way]
        return self.buf.at[slot, pl.ds(lo, n)]

    def relay(self, way):
        me, dx = self.me, (1, -1)[way]
        slot = (me.x - dx) % 4
        arrived(self.buf.at[slot], self.rs.at[way])
        block = self.part(slot, way)
        self.sends.start(block, block, self.ss.at[2 + way], self.rs.at[2 + way], me.at(dx=dx))

    def finish(self):
        for way in range(2):
            arrived(self.part((self.me.x + 2) % 4, way), self.rs.at[2 + way])


class Gather:
    def __init__(self, me, sends, own, buf, sems):
        self.me, self.sends, self.own, self.buf = me, sends, own, buf
        self.zs, self.zr, self.ys, self.yr, self.cs, self.cr = sems

    def start_z(self):
        me = self.me
        dst = self.buf.at[me.y, me.zh % 2, me.c, me.zl]
        recv = self.zr.at[(me.zh % 2) * 2 + me.zl]
        for i in range(4):
            z = me.half + 2 * i
            self.sends.start_unless_self(me, z, self.own, dst, self.zs.at[i], recv, me.at(z=z))

    def to_core(self, slot, r, k):
        me = self.me
        block = self.buf.at[slot, k, me.c]
        self.sends.start(block, block, self.cs.at[r * 2 + k], self.cr.at[r * 2 + k], me.at(c=1 - me.c))

    def start_y(self, k):
        me = self.me
        for s in range(2):
            arrived(self.buf.at[me.y, k, me.c, s], self.zr.at[k * 2 + s])
        block = self.buf.at[me.y, k, me.c]
        for way, dy in enumerate((1, -1)):
            self.sends.start(block, block, self.ys.at[way * 2 + k], self.yr.at[way * 2 + k], me.at(dy=dy))
        self.to_core(me.y, 0, k)

    def near(self, way, k):
        me, dy = self.me, (1, -1)[way]
        slot = (me.y - dy) % 4
        block = self.buf.at[slot, k, me.c]
        arrived(block, self.yr.at[way * 2 + k])
        if way == k:
            self.sends.start(block, block, self.ys.at[4 + way], self.yr.at[4 + way], me.at(dy=dy))
        self.to_core(slot, 1 + way, k)

    def far(self, k):
        slot = (self.me.y + 2) % 4
        arrived(self.buf.at[slot, k, self.me.c], self.yr.at[4 + k])
        self.to_core(slot, 3, k)

    def from_core(self):
        me = self.me
        for r, off in enumerate(OFFSETS):
            for k in range(2):
                arrived(self.buf.at[(me.y + off) % 4, k, 1 - me.c], self.cr.at[r * 2 + k])


class Scatter:
    def __init__(self, me, sends, compute, acc, bufs, sems):
        self.me, self.sends, self.compute, self.acc = me, sends, compute, acc
        self.pst, self.prv, self.fst, self.frv, self.nst, self.nrv, self.zst, self.zrv = bufs
        self.cs, self.cr, self.ys, self.yr, self.zs, self.zr = sems

    def index(self, i):
        r = 3 - i // 2
        off = jnp.where(r == 0, 0, jnp.where(r == 1, 3, jnp.where(r == 2, 1, 2)))
        return r * 2 + i % 2, (self.me.y + off) % 4, i % 2

    def to_core(self):
        me = self.me

        def step(i, _):
            s, slot, k = self.index(i)
            self.pst[s] = self.compute(slot, k, 1 - me.c).astype(BF16)
            rcopy(self.pst.at[s], self.prv.at[s], self.cs.at[s], self.cr.at[s], me.at(c=1 - me.c)).start()
            return 0

        lax.fori_loop(0, 8, step, 0)

        def finish():
            def step(s, _):
                rcopy(self.pst.at[s], self.prv.at[s], self.cs.at[s], self.cr.at[s], me.at(c=1 - me.c)).wait_send()
                return 0

            lax.fori_loop(0, 8, step, 0)

        self.sends.waits.append(finish)

    def from_core(self):
        me = self.me

        def step(i, _):
            s, slot, k = self.index(i)
            arrived(self.prv.at[s], self.cr.at[s])
            self.acc[s] = self.compute(slot, k, me.c) + self.prv[s].astype(F32)
            return 0

        lax.fori_loop(0, 8, step, 0)
        for k, dy in enumerate((1, -1)):
            self.fst[k] = self.acc[6 + k].astype(BF16)
            self.sends.start(self.fst.at[k], self.frv.at[k], self.ys.at[4 + k], self.yr.at[4 + k], me.at(dy=dy))
        for way in range(2):
            self.to_near(way, 1 - way, False)

    def to_near(self, way, k, add):
        me, dy = self.me, (1, -1)[way]
        r = 2 - way
        s = way * 2 + k
        value = self.acc[r * 2 + k]
        if add:
            arrived(self.frv.at[way], self.yr.at[4 + way])
            value = value + self.frv[way].astype(F32)
        self.nst[s] = value.astype(BF16)
        self.sends.start(self.nst.at[s], self.nrv.at[s], self.ys.at[s], self.yr.at[s], me.at(dy=dy))

    def relay(self):
        for way in range(2):
            self.to_near(way, way, True)

    def keep(self, own):
        for k in range(2):
            own[k] = self.acc[k]
        self.own = own

    def start_z(self, k):
        me = self.me
        m = self.zst.shape[1]
        total = self.own[k]
        for way in range(2):
            s = way * 2 + k
            arrived(self.nrv.at[s], self.yr.at[s])
            total = total + self.nrv[s].astype(F32)
        total = total.astype(BF16)
        for l in range(2):
            s = k * 2 + l
            self.zst[s] = total[l * m : (l + 1) * m]
            z = 4 * me.zl + s
            self.sends.start_unless_self(
                me, z, self.zst.at[s], self.zrv.at[me.zh], self.zs.at[s], self.zr.at[me.zh], me.at(z=z)
            )

    def total(self):
        value = None
        for s in range(4):
            arrived(self.zrv.at[s], self.zr.at[s])
            term = self.zrv[s].astype(F32)
            value = term if value is None else value + term
        return value


def kernel(
    text, grad_out, vision, gate, w_query, w_key, w_value, w_out, update, grad_text, grad_vision,
    wkv_g, wq_g, wo_g, text_g, grad_g, kvg_g, vis_g,
    q_acc, q_st, q_rv, att_g, dq_g, ag_acc, ag_st, ag_rv, gv_acc, gv_st, gv_rv, jg, kv_all, kvp, kvp_rv,
    probs_s, expo_acc, acc, acc_kv, own_o, own_t, own_v,
    *rest,
):
    o_bufs, t_bufs, v_bufs = rest[0:8], rest[8:16], rest[16:24]
    rest = rest[24:]
    x_sems = [rest[2 * i : 2 * i + 2] for i in range(3)]
    rest = rest[6:]
    g_sems = [rest[6 * i : 6 * i + 6] for i in range(3)]
    rest = rest[18:]
    r_sems = [rest[6 * i : 6 * i + 6] for i in range(3)]
    rest = rest[18:]
    e_ss, e_rs, m_ss, m_rs, n_ss, n_rs, l_sem = rest

    me = Here()
    sends = Sends()
    zp = me.zl + 2 * me.zh + 1 - 2 * me.zl
    piece = (me.zh % 2) * 2 + me.c

    def exchange(i, src, dst):
        sends.start(src, dst, e_ss.at[i], e_rs.at[i], me.at(z=zp))

    def mate(j):
        p = (piece + 1 + j) % 4
        return p, me.at(z=me.half * 4 + (p // 2) * 2 + me.zl, c=p % 2)

    barrier = pltpu.get_barrier_semaphore()
    around = [me.at(dx=1), me.at(dx=-1), me.at(dy=1), me.at(dy=-1), me.at(z=zp)]
    around += [mate(j)[1] for j in range(3)]
    for device in around:
        pl.semaphore_signal(barrier, inc=1, device_id=device, device_id_type=MESH)
    for i in range(4):
        for z in (me.half + 2 * i, 4 * me.zl + i):

            @pl.when(z != me.z)
            def _():
                pl.semaphore_signal(barrier, inc=1, device_id=me.at(z=z), device_id_type=MESH)

    pl.semaphore_wait(barrier, jnp.where(me.zl == me.half, 14, 16))

    gx_kv = RingGather(me, sends, wkv_g.at[me.x], wkv_g, 128, x_sems[0])
    gx_q = RingGather(me, sends, w_query, wq_g, 512, x_sems[1])
    gx_o = RingGather(me, sends, w_out, wo_g, 128, x_sems[2])
    g_text = Gather(me, sends, text, text_g, g_sems[0])
    g_grad = Gather(me, sends, grad_out, grad_g, g_sems[1])
    g_kv = Gather(me, sends, jg, kvg_g, g_sems[2])

    wkv_g[me.x, :, :HEAD] = w_key[...]
    wkv_g[me.x, :, HEAD:] = w_value[...]
    gx_kv.start()
    exchange(0, vision, vis_g.at[:, me.zl])
    g_text.start_z()
    gx_q.start()
    g_grad.start_z()
    gx_o.start()
    locals_ = [
        pltpu.make_async_copy(vision, vis_g.at[:, me.zl], l_sem.at[0]),
        pltpu.make_async_copy(w_query, wq_g.at[me.x], l_sem.at[1]),
        pltpu.make_async_copy(w_out, wo_g.at[me.x], l_sem.at[2]),
    ]
    for copy in locals_:
        copy.start()

    def kv_block(slot, k, cc):
        rows = vis_g[k * 2 + cc].reshape(128, vis_g.shape[3])
        return dot(rows, wkv_g[slot])

    gx_kv.relay(0)
    gx_kv.relay(1)
    g_text.start_y(0)
    g_text.start_y(1)
    locals_[0].wait()
    arrived(vis_g.at[:, 1 - me.zl], e_rs.at[0])
    gx_kv.finish()
    s_kv = Scatter(me, sends, kv_block, acc_kv, v_bufs, r_sems[2])
    s_kv.to_core()
    s_kv.from_core()
    s_kv.keep(own_v)
    gx_q.relay(0)
    gx_q.relay(1)
    s_kv.relay()
    g_text.near(0, 0)
    g_text.near(1, 1)
    g_text.near(0, 1)
    g_text.near(1, 0)
    gx_o.relay(0)
    gx_o.relay(1)
    g_grad.start_y(0)
    g_grad.start_y(1)
    s_kv.start_z(0)
    s_kv.start_z(1)
    g_text.far(0)
    g_text.far(1)

    projected = s_kv.total()
    keys = projected[:, :HEAD]
    key_scale = lax.rsqrt(jnp.mean(keys * keys, axis=-1, keepdims=True) + EPS)
    kv_all[piece, :, :HEAD] = (keys * key_scale).astype(BF16)
    kv_all[piece, :, HEAD:] = projected[:, HEAD:].astype(BF16)
    own_v[0, :64] = projected
    for j in range(3):
        p, device = mate(j)
        sends.start(kv_all.at[piece], kv_all.at[piece], m_ss.at[j], m_rs.at[piece], device)

    g_text.from_core()
    gx_q.finish()
    locals_[1].wait()
    q_acc[...] = jnp.zeros_like(q_acc)

    def q_step(i, _):
        rows = text_g[i // 4, (i % 4) // 2, i % 2].reshape(512, 256)
        block = wq_g[i // 4, pl.ds(pl.multiple_of((i % 4) * 256, 256), 256), :]
        q_acc[...] += dot(rows, block).reshape(2, 256, 256)
        return 0

    lax.fori_loop(0, 16, q_step, 0)
    q_st[...] = q_acc[1 - me.zl].astype(BF16)
    exchange(1, q_st, q_rv)

    g_grad.near(0, 0)
    g_grad.near(1, 1)
    g_grad.near(0, 1)
    g_grad.near(1, 0)

    for j in range(3):
        p, _ = mate(j)
        arrived(kv_all.at[p], m_rs.at[p])
    kv = kv_all[...].reshape(256, 256)
    key_head, value_head = kv[:, :HEAD], kv[:, HEAD:]
    scale = HEAD ** (-0.5)
    tanh_gate = jnp.tanh(gate[...])

    arrived(q_rv, e_rs.at[1])
    query = q_acc[me.zl] + q_rv[...].astype(F32)
    q_acc[0] = query
    for h in range(2):
        q = query[:, h * HEAD : (h + 1) * HEAD]
        q_scale = lax.rsqrt(jnp.mean(q * q, axis=-1, keepdims=True) + EPS)
        q_normed = (q * q_scale).astype(BF16)
        expo = jnp.exp(dot(q_normed, key_head, NT) * scale)
        probs = expo / jnp.sum(expo, axis=-1, keepdims=True)
        expo_acc[h] = probs
        low = probs.astype(BF16)
        probs_s[h] = low
        att_g[me.zl, :, h * HEAD : (h + 1) * HEAD] = dot(low, value_head).astype(BF16)
    exchange(2, att_g.at[me.zl], att_g.at[me.zl])
    g_grad.far(0)
    g_grad.far(1)

    gx_o.finish()
    locals_[2].wait()

    def out_block(slot, k, cc):
        block = wo_g[slot, :, pl.ds(pl.multiple_of((k * 2 + cc) * 256, 256), 256)]
        return dot(att_g[...].reshape(512, 256), block)

    arrived(att_g.at[1 - me.zl], e_rs.at[2])
    s_out = Scatter(me, sends, out_block, acc, o_bufs, r_sems[0])
    s_out.to_core()
    s_out.from_core()
    s_out.keep(own_o)

    g_grad.from_core()
    ag_acc[...] = jnp.zeros_like(ag_acc)

    def ag_step(i, _):
        rows = grad_g[i // 4, (i % 4) // 2, i % 2].reshape(512, 256)
        block = wo_g[i // 4, :, pl.ds(pl.multiple_of((i % 4) * 256, 256), 256)]
        ag_acc[...] += dot(rows, block, NT).reshape(2, 256, 256)
        return 0

    lax.fori_loop(0, 16, ag_step, 0)
    ag_st[...] = ag_acc[1 - me.zl].astype(BF16)
    exchange(3, ag_st, ag_rv)
    s_out.relay()
    arrived(ag_rv, e_rs.at[3])
    attend_grad = (tanh_gate * (ag_acc[me.zl] + ag_rv[...].astype(F32))).astype(BF16)
    key_part = jnp.zeros((256, HEAD), F32)
    value_part = jnp.zeros((256, HEAD), F32)
    for h in range(2):
        q = q_acc[0, :, h * HEAD : (h + 1) * HEAD]
        q_scale = lax.rsqrt(jnp.mean(q * q, axis=-1, keepdims=True) + EPS)
        q_normed = (q * q_scale).astype(BF16)
        a_grad = attend_grad[:, h * HEAD : (h + 1) * HEAD]
        probs = expo_acc[h]
        prob_grad = dot(a_grad, value_head, NT)
        delta = jnp.sum(probs * prob_grad, axis=-1, keepdims=True)
        score_grad = (probs * (prob_grad - delta) * scale).astype(BF16)
        normed_grad = dot(score_grad, key_head)
        mean = jnp.mean(normed_grad * q, axis=-1, keepdims=True)
        q_grad = q_scale * normed_grad - q * (q_scale * q_scale * q_scale) * mean
        dq_g[me.zl, :, h * HEAD : (h + 1) * HEAD] = q_grad.astype(BF16)
        key_part = key_part + dot(score_grad, q_normed, TN)
        value_part = value_part + dot(probs_s[h], a_grad, TN)
    exchange(4, dq_g.at[me.zl], dq_g.at[me.zl])
    kvp[:, :, :HEAD] = key_part.astype(BF16).reshape(4, 64, HEAD)
    kvp[:, :, HEAD:] = value_part.astype(BF16).reshape(4, 64, HEAD)
    for j in range(3):
        p, device = mate(j)
        sends.start(kvp.at[p], kvp_rv.at[piece], n_ss.at[j], n_rs.at[piece], device)

    kv_grad = kvp[piece].astype(F32)
    for j in range(3):
        p, _ = mate(j)
        arrived(kvp_rv.at[p], n_rs.at[p])
        kv_grad = kv_grad + kvp_rv[p].astype(F32)
    keys = own_v[0, :64, :HEAD]
    key_scale = lax.rsqrt(jnp.mean(keys * keys, axis=-1, keepdims=True) + EPS)
    k_grad = kv_grad[:, :HEAD]
    mean = jnp.mean(k_grad * keys, axis=-1, keepdims=True)
    k_grad = key_scale * k_grad - keys * (key_scale * key_scale * key_scale) * mean
    jg[:, :HEAD] = k_grad.astype(BF16)
    jg[:, HEAD:] = kv_grad[:, HEAD:].astype(BF16)
    g_kv.start_z()

    def text_block(slot, k, cc):
        block = wq_g[slot, pl.ds(pl.multiple_of((k * 2 + cc) * 256, 256), 256), :]
        return dot(dq_g[...].reshape(512, 256), block, NT)

    arrived(dq_g.at[1 - me.zl], e_rs.at[4])
    s_text = Scatter(me, sends, text_block, acc, t_bufs, r_sems[1])
    s_text.to_core()
    s_text.from_core()
    s_text.keep(own_t)
    s_out.start_z(0)
    s_out.start_z(1)
    g_kv.start_y(0)
    g_kv.start_y(1)
    s_text.relay()
    g_kv.near(0, 0)
    g_kv.near(1, 1)
    g_kv.near(0, 1)
    g_kv.near(1, 0)
    update[...] = (tanh_gate * s_out.total()).astype(BF16)
    g_kv.far(0)
    g_kv.far(1)
    g_kv.from_core()

    gv_acc[...] = jnp.zeros_like(gv_acc)

    def gv_step(i, _):
        rows = kvg_g[i].reshape(512, 256)
        gv_acc[...] += dot(rows, wkv_g[i], NT).reshape(4, 2, 64, -1)
        return 0

    lax.fori_loop(0, 4, gv_step, 0)
    gv_st[...] = gv_acc[:, 1 - me.zl].astype(BF16)
    exchange(5, gv_st, gv_rv)
    s_text.start_z(0)
    s_text.start_z(1)
    arrived(gv_rv, e_rs.at[5])
    grad_vision[...] = (gv_acc[:, me.zl] + gv_rv[...].astype(F32)).astype(BF16)
    grad_text[...] = s_text.total().astype(BF16)
    sends.finish()


def body(text, grad_out, vision, gate, w_query, w_key, w_value, w_out):
    features = vision.shape[1]
    dma = lambda n: pltpu.SemaphoreType.DMA((n,))
    vm = pltpu.VMEM

    def scatter_bufs(m):
        return [
            vm((8, 2 * m, 256), BF16), vm((8, 2 * m, 256), BF16),
            vm((2, 2 * m, 256), BF16), vm((2, 2 * m, 256), BF16),
            vm((4, 2 * m, 256), BF16), vm((4, 2 * m, 256), BF16),
            vm((4, m, 256), BF16), vm((4, m, 256), BF16),
        ]

    scratch = [
        vm((4, features, 256), BF16), vm((4, 1024, 256), BF16), vm((4, 256, 1024), BF16),
        vm((4, 2, 2, 2, 256, 256), BF16), vm((4, 2, 2, 2, 256, 256), BF16), vm((4, 2, 2, 2, 64, 256), BF16),
        vm((4, 2, 64, features), BF16),
        vm((2, 256, 256), F32), vm((256, 256), BF16), vm((256, 256), BF16),
        vm((2, 256, 256), BF16), vm((2, 256, 256), BF16),
        vm((2, 256, 256), F32), vm((256, 256), BF16), vm((256, 256), BF16),
        vm((4, 2, 64, features), F32), vm((4, 64, features), BF16), vm((4, 64, features), BF16),
        vm((64, 256), BF16), vm((4, 64, 256), BF16), vm((4, 64, 256), BF16), vm((4, 64, 256), BF16),
        vm((2, 256, 256), BF16), vm((2, 256, 256), F32),
        vm((8, 512, 256), F32), vm((8, 128, 256), F32),
        vm((2, 512, 256), F32), vm((2, 512, 256), F32), vm((2, 128, 256), F32),
    ]
    scratch += scatter_bufs(256) + scatter_bufs(256) + scatter_bufs(64)
    scratch += [dma(4), dma(4)] * 3
    scratch += [dma(4), dma(4), dma(6), dma(6), dma(8), dma(8)] * 3
    scratch += [dma(8), dma(8), dma(6), dma(6), dma(4), dma(4)] * 3
    scratch += [dma(6), dma(6), dma(3), dma(4), dma(3), dma(4), dma(3)]
    whole = pl.BlockSpec(memory_space=pltpu.VMEM)
    update, grad_text, grad_vision = pl.pallas_call(
        kernel,
        out_shape=(
            jax.ShapeDtypeStruct((256, 256), BF16),
            jax.ShapeDtypeStruct((256, 256), BF16),
            jax.ShapeDtypeStruct((4, 64, features), BF16),
        ),
        in_specs=[whole] * 8,
        out_specs=(whole,) * 3,
        scratch_shapes=scratch,
        name="cross_attention",
        compiler_params=pltpu.CompilerParams(
            collective_id=0, has_side_effects=True, vmem_limit_bytes=60 * 2**20
        ),
    )(
        text, grad_out, vision.reshape(4, 64, features), gate.reshape(1, 1),
        w_query, w_key, w_value, w_out,
    )
    return update, grad_text, grad_vision.reshape(256, features)


def solution(mesh):
    return jax.shard_map(
        body,
        mesh=mesh,
        in_specs=(
            P("dp", "tensor"), P("dp", "tensor"), P("dp", "tensor"), P(),
            P("dp", "tensor"), P("tensor", "dp"), P("tensor", "dp"), P("tensor", "dp"),
        ),
        out_specs=(P("dp", "tensor"), P("dp", "tensor"), P("dp", "tensor")),
        check_vma=False,
    )
```

time: 887 us -> 161 us (0.18)
  waiting for transfers between devices: 785 us -> 0 us
  Pallas kernels: 0 us -> 155 us
  blocking collectives: 45.5 us -> 0 us
  matrix products: 25.6 us -> 0 us
  between operations: 15.1 us -> 1.3 us
    all_gather x6 -> x0, waiting for transfers between devices: 404 us -> none  [the longest x1 90.5 us: body(): lax.all_gather(w_query, 'dp', axis=0, tiled=True)]
    reduce_scatter x2 -> x0, waiting for transfers between devices: 197 us -> none  [the longest x1 100 us: body(): lax.psum_scatter(input_part.astype(jnp.bfloat16), 'tensor', scatter_dimen...]
    unnamed x12 -> x0, waiting for transfers between devices: 184 us -> none
    pallas_call x0 -> x1, Pallas kernels: none -> 155 us  [body(): pl.pallas_call(kernel, out_shape=(jax.ShapeDtypeStruct((256, 256), BF16),...]
    all_gather x2 -> x0, blocking collectives: 45.5 us -> none  [the longest x1 23.6 us: body(): lax.all_gather(w_key, 'dp', axis=1, tiled=True)]
    dot_general x12 -> x0, matrix products: 25.4 us -> none  [the longest x1 5.47 us: body(): jnp.einsum('tk,dk->td', query_grad, query_w, preferred_element_type=jnp.f...]
  transfers between devices with their start and end apart: 10 -> 0, of which waited for: 10 -> 0; matrix products, arithmetic and copies ran while one was open for 3% -> 0% of each run, Pallas kernels for 0% -> 0%
where the time goes in v1:
time: 161 us
  Pallas kernels  155 us (96%)
  local copies, waits for them, and re-layouts  4.96 us (3%)
    pallas_call x1, Pallas kernels, body(): pl.pallas_call(kernel, out_shape=(jax.ShapeDtypeStruct((256, 256), BF16),...  155 us
    unnamed x8, local copies, waits for them, and re-layouts  4.96 us

profile of v1, /device:TPU:1, one launch (start us, length us, event | category | flops | bytes accessed | tf_op | source)
XLA Modules:
  0.0 161.0 jit_solution(12013920476583350198)
XLA Ops:
  1.3 1.7 %copy.11 = bf16[256,240]{1,0:T(8,128)(2,1)} copy(bf16[256,240]{0,1:T(8,128)(2,1)} %param.10) | data formatting | bytes 245760 | tf_op args[2]
  2.9 154.7 %cross_attention.1 = (bf16[256,256]{1,0:T(8,128)(2,1)}, bf16[256,256]{1,0:T(8,128)(2,1)}, bf16[4,64,240]{2,1,0:T(8,128)(2,1)}) custom-call(bf16[256,256]{1,0:T(8,128)(2,1)} %text.1, bf16[256,256]{1,0:T(8,128)(2,1)} %grad_out.1, bf16[4,64,240]{2,1,0:T(8,128)(2,1)} %bitcast.4, f32[1,1]{1,0:T(1,128)} %bitcast.3.gate, bf16[1024,256]{1,0:T(8,128)(2,1)} %w_query.1, ...), custom_call_target="tpu_custom_call" | custom-call | tf_op jit(solution)/shard_map/cross_attention/pallas_call | solution.py:537
  157.7 0.0 copy-start.1
  157.7 1.7 %copy.12 = bf16[256,240]{0,1:T(8,128)(2,1)} copy(bf16[256,240]{1,0:T(8,128)(2,1)} %bitcast.5) | data formatting | bytes 245760
  159.4 0.0 copy-done.1
  159.4 0.0 copy-start
  159.4 0.7 copy.16
  160.0 0.3 copy-done
  160.3 0.7 copy.17
Async XLA Ops:
  157.7 1.7 %copy-start.1 = (bf16[256,256]{1,0:T(8,128)(2,1)S(1)}, bf16[256,256]{1,0:T(8,128)(2,1)}, u32[]{:S(2)}) copy-start(bf16[256,256]{1,0:T(8,128)(2,1)} %get-tuple-element.15) | copy-start | bytes 393220
  159.4 1.0 copy-start

commit v2 on v1

v2 whole, which is shorter than its diff:
```python
import jax
import jax.numpy as jnp
from jax import lax
from jax.experimental import pallas as pl
from jax.experimental.pallas import tpu as pltpu
from jax.sharding import PartitionSpec as P

HEAD = 128
EPS = 1e-05
MESH = pl.DeviceIdType.MESH
F32 = jnp.float32
BF16 = jnp.bfloat16
OFFSETS = (0, 3, 1, 2)
NT = (((1,), (1,)), ((), ()))
TN = (((0,), (0,)), ((), ()))


def dot(a, b, dims=(((1,), (0,)), ((), ()))):
    return lax.dot_general(a, b, dims, preferred_element_type=F32)


class Here:
    def __init__(self):
        d, t = lax.axis_index("dp"), lax.axis_index("tensor")
        self.x, self.zl = d // 2, d % 2
        self.y, self.zh, self.c = t // 8, (t // 2) % 4, t % 2
        self.z = 2 * self.zh + self.zl
        self.half = self.zh // 2
        self.kept = self.zl == self.half
        self.place = jnp.where(self.zl == 0, self.z, 7 - self.z) // 2
        self.next_z = (self.z + jnp.where(self.place == 2, 2, -2) * (1 - 2 * self.zl)) % 8
        self.toward = 1 - 2 * self.half

    def order(self, i):
        u = self.place
        table = ((0, 1, 2, 3), (2, 1, 3, 0), (3, 2, 0, 1), (0, 1, 2, 3))
        j = table[3][i]
        for n in (2, 1, 0):
            j = jnp.where(u == n, table[n][i], j)
        return jnp.where(self.zl == 0, j, 3 - j)

    def at(self, dx=0, dy=0, z=None, c=None):
        x = (self.x + dx) % 4 if dx else self.x
        y = (self.y + dy) % 4 if dy else self.y
        z = self.z if z is None else z
        c = self.c if c is None else c
        return (x * 2 + z % 2, y * 8 + (z // 2) * 2 + c)


def rcopy(src, dst, send, recv, device):
    return pltpu.make_async_remote_copy(
        src_ref=src, dst_ref=dst, send_sem=send, recv_sem=recv, device_id=device, device_id_type=MESH
    )


class Sends:
    def __init__(self):
        self.waits = []

    def start(self, *args):
        copy = rcopy(*args)
        copy.start()
        self.waits.append(copy.wait_send)

    def start_unless_self(self, me, z, src, dst, send, recv, device):
        @pl.when(z != me.z)
        def _():
            rcopy(src, dst, send, recv, device).start()

        @pl.when(z == me.z)
        def _():
            pltpu.make_async_copy(src, dst, recv).start()

        def finish():
            @pl.when(z != me.z)
            def _():
                rcopy(src, dst, send, recv, device).wait_send()

        self.waits.append(finish)

    def finish(self):
        for wait in self.waits:
            wait()


def arrived(dst, sem):
    pltpu.make_async_copy(dst, dst, sem).wait()


class RingGather:
    def __init__(self, me, sends, own, buf, cut, sems):
        self.me, self.sends, self.own, self.buf, self.cut = me, sends, own, buf, cut
        self.ss, self.rs = sems

    def start(self):
        me = self.me
        for way, dx in enumerate((1, -1)):
            self.sends.start(self.own, self.buf.at[me.x], self.ss.at[way], self.rs.at[way], me.at(dx=dx))

    def part(self, slot, way):
        rows = self.buf.shape[1]
        lo, n = ((0, self.cut), (self.cut, rows - self.cut))[way]
        return self.buf.at[slot, pl.ds(lo, n)]

    def relay(self, way):
        me, dx = self.me, (1, -1)[way]
        slot = (me.x - dx) % 4
        arrived(self.buf.at[slot], self.rs.at[way])
        block = self.part(slot, way)
        self.sends.start(block, block, self.ss.at[2 + way], self.rs.at[2 + way], me.at(dx=dx))

    def finish(self):
        for way in range(2):
            arrived(self.part((self.me.x + 2) % 4, way), self.rs.at[2 + way])


class Gather:
    def __init__(self, me, sends, own, buf, sems):
        self.me, self.sends, self.own, self.buf = me, sends, own, buf
        self.zs, self.zr, self.ys, self.yr, self.cs, self.cr = sems

    def start_z(self, later=False):
        me = self.me
        dst = self.buf.at[me.y, me.zh % 2, me.c, me.zl]
        recv = self.zr.at[(me.zh % 2) * 2 + me.zl]
        one = me.toward * jnp.where(me.kept, -2, 1)
        args = [
            (self.own, dst, self.zs.at[i], recv, me.at(z=(me.z + sign * one) % 8)) for i, sign in enumerate((1, -1))
        ]
        self.sends.start(*args[0])
        self.sends.waits.append(rcopy(*args[1]).wait_send)

        def second():
            rcopy(*args[1]).start()

        @pl.when(me.kept)
        def _():
            pltpu.make_async_copy(self.own, dst, recv).start()

        if not later:
            second()
            return None

        pl.when(jnp.logical_not(me.kept))(second)
        return lambda: pl.when(me.kept)(second)

    def relay_z(self, i):
        if i == 3:
            return
        me = self.me
        cond = (me.place >= 2, me.place != 1, me.place == 1)[i]
        block, sem = self.block(me.y, i), self.zs.at[2 + i % 2]
        args = block, block, sem, self.zr.at[me.order(i)], me.at(z=me.next_z)

        @pl.when(cond)
        def _():
            rcopy(*args).start()

        def finish():
            @pl.when(cond)
            def _():
                rcopy(*args).wait_send()

        self.sends.waits.append(finish)

    def block(self, slot, i):
        j = self.me.order(i)
        return self.buf.at[slot, j // 2, self.me.c, j % 2]

    def to_core(self, slot, r, i):
        block = self.block(slot, i)
        rcopy(block, block, self.cs.at[0], self.cr.at[r], self.me.at(c=1 - self.me.c)).start()

    def arrive(self, *positions):
        for i in positions:
            arrived(self.block(self.me.y, i), self.zr.at[self.me.order(i)])
            self.relay_z(i)

    def start_y(self, *positions):
        me = self.me
        for i in positions:
            block = self.block(me.y, i)
            for way, dy in enumerate((1, -1)):
                rcopy(block, block, self.ys.at[way], self.yr.at[way * 4 + i], me.at(dy=dy)).start()
            self.to_core(me.y, 0, i)

    def near(self, *positions):
        me = self.me
        for i in positions:
            for way, dy in enumerate((1, -1)):
                slot = (me.y - dy) % 4
                block = self.block(slot, i)
                arrived(block, self.yr.at[way * 4 + i])
                if way == i % 2:
                    rcopy(block, block, self.ys.at[2 + way], self.yr.at[8 + i], me.at(dy=dy)).start()
                self.to_core(slot, 1 + way, i)

    def far(self, *positions):
        slot = (self.me.y + 2) % 4
        for i in positions:
            arrived(self.block(slot, i), self.yr.at[8 + i])
            self.to_core(slot, 3, i)

    def from_core(self, *rs):
        me = self.me
        for r in rs:
            arrived(self.buf.at[(me.y + OFFSETS[r]) % 4, :, 1 - me.c], self.cr.at[r])
        if 3 in rs:
            self.sends.waits.append(self.sent)

    def sent(self):
        c = self.me.c
        arrived(self.buf.at[:, :, c], self.cs.at[0])
        for way in range(2):
            arrived(self.buf.at[0, :, c], self.ys.at[way])
            arrived(self.buf.at[0, 0, c], self.ys.at[2 + way])


class Scatter:
    def __init__(self, me, sends, compute, acc, bufs, sems):
        self.me, self.sends, self.compute, self.acc = me, sends, compute, acc
        self.pst, self.prv, self.fst, self.frv, self.nst, self.nrv, self.zst, self.zrv = bufs
        self.cs, self.cr, self.ys, self.yr, self.zs, self.zr = sems

    def to_core(self, *rs):
        me = self.me
        for r in rs:

            def step(k, _):
                s = r * 2 + k
                self.pst[s] = self.compute((me.y + OFFSETS[r]) % 4, k, 1 - me.c).astype(BF16)
                rcopy(self.pst.at[s], self.prv.at[s], self.cs.at[0], self.cr.at[r], me.at(c=1 - me.c)).start()
                return 0

            lax.fori_loop(0, 2, step, 0)

    def from_core(self, r):
        me = self.me
        arrived(self.prv.at[pl.ds(r * 2, 2)], self.cr.at[r])

        def step(k, _):
            s = r * 2 + k
            value = self.compute((me.y + OFFSETS[r]) % 4, k, me.c) + self.prv[s].astype(F32)
            self.acc[s] = value.reshape(self.acc.shape[1:])
            return 0

        lax.fori_loop(0, 2, step, 0)

    def mine(self, r, i):
        j = self.me.order(3 - i)
        return self.acc[r * 2 + j // 2, j % 2]

    def send_far(self):
        me = self.me
        self.from_core(3)
        for i in range(4):
            self.fst[i] = self.mine(3, i).astype(BF16)
            self.sends.start(
                self.fst.at[i], self.frv.at[i], self.ys.at[8 + i], self.yr.at[8 + i], me.at(dy=(1, -1)[i % 2])
            )

    def begin(self):
        self.to_core(3)
        self.to_core(2, 1)
        self.send_far()
        self.from_core(2)
        self.near((0, 1))
        self.from_core(1)
        self.near((1, 0))
        self.to_core(0)
        self.sends.waits.append(lambda: arrived(self.pst, self.cs.at[0]))

    def near(self, *items):
        me = self.me
        for way, i in items:
            s = way * 4 + i
            value = self.mine(2 - way, i)
            if i % 2 == way:
                arrived(self.frv.at[i], self.yr.at[8 + i])
                value = value + self.frv[i].astype(F32)
            self.nst[s] = value.astype(BF16)
            self.sends.start(self.nst.at[s], self.nrv.at[s], self.ys.at[s], self.yr.at[s], me.at(dy=(1, -1)[way]))

    def start_z(self, *positions):
        me = self.me
        for i in positions:
            total = self.mine(0, i)
            for way in range(2):
                s = way * 4 + i
                arrived(self.nrv.at[s], self.yr.at[s])
                total = total + self.nrv[s].astype(F32)
            self.zst[i] = total.astype(BF16)
            z = 4 * me.zl + me.order(3 - i)
            self.sends.start_unless_self(
                me, z, self.zst.at[i], self.zrv.at[me.zh], self.zs.at[i], self.zr.at[me.zh], me.at(z=z)
            )

    def total(self):
        value = None
        for s in range(4):
            arrived(self.zrv.at[s], self.zr.at[s])
            term = self.zrv[s].astype(F32)
            value = term if value is None else value + term
        return value


def kernel(
    text, grad_out, vision, gate, w_query, w_key, w_value, w_out, update, grad_text, grad_vision,
    wkv_g, wq_g, wo_g, text_g, grad_g, kvg_g, vis_g, vis_r,
    q_acc, q_st, q_rv, att_g, dq_g, ag_acc, ag_st, ag_rv, gv_acc, gv_st, gv_rv, jg, kv_all, kvp, kvp_rv,
    probs_low, probs, query, query_low, query_scale, attend_grad, score_grad, acc_o, acc_t, acc_v, own_kv,
    *rest,
):
    o_bufs, t_bufs, v_bufs = rest[0:8], rest[8:16], rest[16:24]
    rest = rest[24:]
    x_sems = [rest[2 * i : 2 * i + 2] for i in range(3)]
    rest = rest[6:]
    g_sems = [rest[6 * i : 6 * i + 6] for i in range(3)]
    rest = rest[18:]
    r_sems = [rest[6 * i : 6 * i + 6] for i in range(3)]
    rest = rest[18:]
    e_ss, e_rs, m_ss, m_rs, n_ss, n_rs, l_sem = rest

    me = Here()
    sends = Sends()
    zp = me.zl + 2 * me.zh + 1 - 2 * me.zl
    piece = (me.zh % 2) * 2 + me.c
    near_y = [(me.y + off) % 4 for off in OFFSETS]

    def exchange(i, src, dst):
        sends.start(src, dst, e_ss.at[i], e_rs.at[i], me.at(z=zp))

    def mate(j):
        p = (piece + 1 + j) % 4
        return p, me.at(z=me.half * 4 + (p // 2) * 2 + me.zl, c=p % 2)

    gx_kv = RingGather(me, sends, wkv_g.at[me.x], wkv_g, 128, x_sems[0])
    gx_q = RingGather(me, sends, w_query, wq_g, 512, x_sems[1])
    gx_o = RingGather(me, sends, w_out, wo_g, 128, x_sems[2])
    g_text = Gather(me, sends, text, text_g, g_sems[0])
    g_grad = Gather(me, sends, grad_out, grad_g, g_sems[1])
    g_kv = Gather(me, sends, jg, kvg_g, g_sems[2])

    barrier = pltpu.get_barrier_semaphore()
    around = [me.at(dx=1), me.at(dx=-1), me.at(dy=1), me.at(dy=-1), me.at(z=zp)]
    around += [mate(j)[1] for j in range(3)]
    for device in around:
        pl.semaphore_signal(barrier, inc=1, device_id=device, device_id_type=MESH)
    for i in range(4):
        for z in (me.half + 2 * i, 4 * me.zl + i):

            @pl.when(z != me.z)
            def _():
                pl.semaphore_signal(barrier, inc=1, device_id=me.at(z=z), device_id_type=MESH)

    @pl.when(jnp.logical_not(me.kept))
    def _():
        pl.semaphore_signal(barrier, inc=1, device_id=me.at(z=me.next_z), device_id_type=MESH)

    local_q = pltpu.make_async_copy(w_query, wq_g.at[me.x], l_sem.at[0])
    local_o = pltpu.make_async_copy(w_out, wo_g.at[me.x], l_sem.at[1])
    local_q.start()
    local_o.start()
    wkv_g[me.x, :, :HEAD] = w_key[...]
    wkv_g[me.x, :, HEAD:] = w_value[...]
    pl.semaphore_wait(barrier, jnp.where(me.kept, 14, 17))

    second = g_text.start_z(later=True)
    gx_kv.start()
    exchange(0, vision, vis_g)

    def kv_block(slot, k, cc):
        return dot(vis_r[k * 2 + cc].reshape(128, vis_r.shape[3]), wkv_g[slot])

    @pl.when(me.kept)
    def _():
        arrived(g_text.block(me.y, 0), g_text.zr.at[me.order(0)])
        g_text.start_y(0)

    vis_r[:, me.zl] = vision[...].T.reshape(4, 64, -1)
    gx_kv.relay(0)
    gx_kv.relay(1)
    gx_q.start()
    second()

    @pl.when(jnp.logical_not(me.kept))
    def _():
        arrived(g_text.block(me.y, 0), g_text.zr.at[me.order(0)])
        g_text.start_y(0)

    g_text.relay_z(0)
    g_text.arrive(1)
    g_text.start_y(1)
    g_text.near(0)
    g_text.arrive(2)
    g_text.start_y(2)
    with jax.named_scope("vis_wait"):
        arrived(vis_g, e_rs.at[0])
    vis_r[:, 1 - me.zl] = vis_g[...].T.reshape(4, 64, -1)
    gx_kv.finish()
    s_kv = Scatter(me, sends, kv_block, acc_v, v_bufs, r_sems[2])
    s_kv.to_core(3, 2, 1, 0)
    g_text.arrive(3)
    g_text.start_y(3)
    g_grad.start_z()
    s_kv.send_far()
    g_text.near(1)
    s_kv.from_core(2)
    s_kv.from_core(1)
    s_kv.near((0, 1), (1, 0), (0, 3), (1, 2))
    s_kv.from_core(0)
    sends.waits.append(lambda: arrived(s_kv.pst, s_kv.cs.at[0]))
    g_text.near(2)
    gx_q.relay(0)
    gx_q.relay(1)
    gx_o.start()
    s_kv.near((0, 0), (1, 1), (0, 2), (1, 3))
    g_grad.arrive(0)
    g_text.near(3)
    g_grad.arrive(1)
    g_grad.start_y(0, 1)
    s_kv.start_z(0, 1, 2, 3)

    def q_part(slot):
        total = None
        for j in range(4):
            term = dot(text_g[slot, j // 2, j % 2].reshape(512, 256), wq_g[slot, pl.ds(j * 256, 256), :])
            total = term if total is None else total + term
        return total.reshape(2, 256, 256)

    g_text.far(0, 1, 2, 3)
    g_grad.arrive(2)
    g_grad.start_y(2)
    g_text.from_core(0, 1, 2)
    local_q.wait()
    gx_q.finish()
    with jax.named_scope("query"):
        q_acc[...] = q_part(near_y[0])
        q_acc[...] += q_part(near_y[1])
        q_acc[...] += q_part(near_y[2])
    g_text.from_core(3)
    with jax.named_scope("query_last"):
        q_acc[...] += q_part(near_y[3])
        for h in range(2):
            q_st[h] = q_acc[1 - me.zl, :, h * HEAD : (h + 1) * HEAD].astype(BF16)
            exchange(1 + h, q_st.at[h], q_rv.at[h])
    g_grad.arrive(3)
    g_grad.start_y(3)

    with jax.named_scope("kv"):
        projected = s_kv.total()
        keys = projected[:, :HEAD]
        key_scale = lax.rsqrt(jnp.mean(keys * keys, axis=-1, keepdims=True) + EPS)
        kv_all[piece, :, :HEAD] = (keys * key_scale).astype(BF16)
        kv_all[piece, :, HEAD:] = projected[:, HEAD:].astype(BF16)
        own_kv[...] = projected
        for j in range(3):
            p, device = mate(j)
            sends.start(kv_all.at[piece], kv_all.at[piece], m_ss.at[j], m_rs.at[piece], device)

    g_grad.near(0)
    with jax.named_scope("kv_wait"):
        for j in range(3):
            p, _ = mate(j)
            arrived(kv_all.at[p], m_rs.at[p])
    kv = kv_all[...].reshape(256, 256)
    key_head, value_head = kv[:, :HEAD], kv[:, HEAD:]
    scale = HEAD ** (-0.5)
    tanh_gate = jnp.tanh(gate[...])

    for h in range(2):
        own = slice(h * HEAD, (h + 1) * HEAD)
        with jax.named_scope("q_wait"):
            arrived(q_rv.at[h], e_rs.at[1 + h])
        with jax.named_scope("attention"):
            q = q_acc[me.zl, :, own] + q_rv[h].astype(F32)
            q_scale = lax.rsqrt(jnp.mean(q * q, axis=-1, keepdims=True) + EPS)
            q_normed = (q * q_scale).astype(BF16)
            query[h] = q
            query_low[h] = q_normed
            query_scale[h] = jnp.broadcast_to(q_scale, q.shape)
            expo = jnp.exp(dot(q_normed, key_head, NT) * scale)
            prob = expo / jnp.sum(expo, axis=-1, keepdims=True)
            probs[h] = prob
            low = prob.astype(BF16)
            probs_low[h] = low
            att_g[me.zl, :, own] = dot(low, value_head).astype(BF16)
            exchange(3 + h, att_g.at[me.zl, :, own], att_g.at[me.zl, :, own])
    g_grad.near(1, 2)
    gx_o.relay(0)
    gx_o.relay(1)
    g_grad.near(3)

    def ag_part(slot):
        total = None
        for j in range(4):
            term = dot(grad_g[slot, j // 2, j % 2].reshape(512, 256), wo_g[slot, :, pl.ds(j * 256, 256)], NT)
            total = term if total is None else total + term
        return total.reshape(2, 256, 256)

    def out_block(slot, k, cc):
        block = wo_g[slot, :, pl.ds(pl.multiple_of((k * 2 + cc) * 256, 256), 256)]
        return dot(att_g[...].reshape(512, 256), block)

    with jax.named_scope("att_wait"):
        for h in range(2):
            theirs = att_g.at[1 - me.zl, :, pl.ds(h * HEAD, HEAD)]
            arrived(theirs, e_rs.at[3 + h])
    s_out = Scatter(me, sends, out_block, acc_o, o_bufs, r_sems[0])
    g_grad.far(0, 1)
    local_o.wait()
    gx_o.finish()
    s_out.begin()
    s_out.near((0, 3), (1, 2))

    g_grad.far(2, 3)
    g_grad.from_core(0, 1, 2)
    with jax.named_scope("attend_grad"):
        ag_acc[...] = ag_part(near_y[0])
        ag_acc[...] += ag_part(near_y[1])
        ag_acc[...] += ag_part(near_y[2])
    g_grad.from_core(3)
    with jax.named_scope("attend_grad_last"):
        ag_acc[...] += ag_part(near_y[3])
        for h in range(2):
            ag_st[h] = ag_acc[1 - me.zl, :, h * HEAD : (h + 1) * HEAD].astype(BF16)
            exchange(5 + h, ag_st.at[h], ag_rv.at[h])
    s_out.from_core(0)
    s_out.near((0, 0), (1, 1))

    for h in range(2):
        own = slice(h * HEAD, (h + 1) * HEAD)
        with jax.named_scope("ag_wait"):
            arrived(ag_rv.at[h], e_rs.at[5 + h])
        with jax.named_scope("backward"):
            a_grad = (tanh_gate * (ag_acc[me.zl, :, own] + ag_rv[h].astype(F32))).astype(BF16)
            attend_grad[h] = a_grad
            prob = probs[h]
            prob_grad = dot(a_grad, value_head, NT)
            delta = jnp.sum(prob * prob_grad, axis=-1, keepdims=True)
            s_grad = (prob * (prob_grad - delta) * scale).astype(BF16)
            score_grad[h] = s_grad
            normed_grad = dot(s_grad, key_head)
            q, q_scale = query[h], query_scale[h]
            mean = jnp.mean(normed_grad * q, axis=-1, keepdims=True)
            q_grad = q_scale * (normed_grad - q * (q_scale * q_scale) * mean)
            dq_g[me.zl, :, own] = q_grad.astype(BF16)
        if h == 0:
            exchange(7, dq_g.at[me.zl, :, own], dq_g.at[me.zl, :, own])
            s_out.near((0, 2), (1, 3))
    with jax.named_scope("kv_part"):
        key_part = dot(score_grad[0], query_low[0], TN) + dot(score_grad[1], query_low[1], TN)
        value_part = dot(probs_low[0], attend_grad[0], TN) + dot(probs_low[1], attend_grad[1], TN)
        kvp[:, :, :HEAD] = key_part.astype(BF16).reshape(4, 64, HEAD)
        kvp[:, :, HEAD:] = value_part.astype(BF16).reshape(4, 64, HEAD)
        for j in range(3):
            p, device = mate(j)
            sends.start(kvp.at[p], kvp_rv.at[piece], n_ss.at[j], n_rs.at[piece], device)
    exchange(8, dq_g.at[me.zl, :, HEAD:], dq_g.at[me.zl, :, HEAD:])

    with jax.named_scope("kv_grad"):
        kv_grad = kvp[piece].astype(F32)
        for j in range(3):
            p, _ = mate(j)
            arrived(kvp_rv.at[p], n_rs.at[p])
            kv_grad = kv_grad + kvp_rv[p].astype(F32)
        keys = own_kv[:, :HEAD]
        key_scale = lax.rsqrt(jnp.mean(keys * keys, axis=-1, keepdims=True) + EPS)
        k_grad = kv_grad[:, :HEAD]
        mean = jnp.mean(k_grad * keys, axis=-1, keepdims=True)
        k_grad = key_scale * k_grad - keys * (key_scale * key_scale * key_scale) * mean
        jg[:, :HEAD] = k_grad.astype(BF16)
        jg[:, HEAD:] = kv_grad[:, HEAD:].astype(BF16)
        g_kv.start_z()

    def text_block(slot, k, cc):
        block = wq_g[slot, pl.ds(pl.multiple_of((k * 2 + cc) * 256, 256), 256), :]
        return dot(dq_g[...].reshape(512, 256), block, NT)

    with jax.named_scope("dq_wait"):
        for h in range(2):
            theirs = dq_g.at[1 - me.zl, :, pl.ds(h * HEAD, HEAD)]
            arrived(theirs, e_rs.at[7 + h])
    s_text = Scatter(me, sends, text_block, acc_t, t_bufs, r_sems[1])
    s_text.to_core(3)
    s_text.to_core(2, 1)
    s_text.send_far()
    g_kv.arrive(0, 1)
    s_text.from_core(2)
    s_text.near((0, 1))
    s_text.from_core(1)
    s_text.near((1, 0))
    s_text.to_core(0)
    sends.waits.append(lambda: arrived(s_text.pst, s_text.cs.at[0]))
    g_kv.arrive(2, 3)
    g_kv.start_y(0, 1, 2, 3)
    s_text.from_core(0)
    s_out.start_z(0, 1, 2, 3)
    s_text.near((0, 0), (1, 1))
    g_kv.near(0, 1, 2, 3)
    s_text.near((0, 2), (1, 2), (0, 3), (1, 3))
    s_text.start_z(0)
    g_kv.far(0, 1, 2, 3)
    g_kv.from_core(0, 1, 2, 3)

    with jax.named_scope("vision_grad"):
        gv = None
        for i in range(4):
            term = dot(kvg_g[i].reshape(512, 256), wkv_g[i], NT)
            gv = term if gv is None else gv + term
        gv_acc[...] = gv.reshape(4, 2, 64, -1)
        gv_st[...] = gv_acc[:, 1 - me.zl].astype(BF16)
        exchange(9, gv_st, gv_rv)
    s_text.start_z(1, 2, 3)
    with jax.named_scope("vision_grad_last"):
        arrived(gv_rv, e_rs.at[9])
        total = gv_acc[:, me.zl] + gv_rv[...].astype(F32)
        grad_vision[...] = total.reshape(256, -1).T.astype(BF16)
    with jax.named_scope("update"):
        update[...] = (tanh_gate * s_out.total()).astype(BF16)
    with jax.named_scope("text_grad_last"):
        grad_text[...] = s_text.total().astype(BF16)
    with jax.named_scope("sends"):
        sends.finish()


def body(text, grad_out, vision, gate, w_query, w_key, w_value, w_out):
    features = vision.shape[1]
    dma = lambda n: pltpu.SemaphoreType.DMA((n,))
    vm = pltpu.VMEM

    def scatter_bufs(m):
        return [
            vm((8, 2 * m, 256), BF16), vm((8, 2 * m, 256), BF16),
            vm((4, m, 256), BF16), vm((4, m, 256), BF16),
            vm((8, m, 256), BF16), vm((8, m, 256), BF16),
            vm((4, m, 256), BF16), vm((4, m, 256), BF16),
        ]

    scratch = [
        vm((4, features, 256), BF16), vm((4, 1024, 256), BF16), vm((4, 256, 1024), BF16),
        vm((4, 2, 2, 2, 256, 256), BF16), vm((4, 2, 2, 2, 256, 256), BF16), vm((4, 2, 2, 2, 64, 256), BF16),
        vm((features, 256), BF16), vm((4, 2, 64, features), BF16),
        vm((2, 256, 256), F32), vm((2, 256, HEAD), BF16), vm((2, 256, HEAD), BF16),
        vm((2, 256, 256), BF16), vm((2, 256, 256), BF16),
        vm((2, 256, 256), F32), vm((2, 256, HEAD), BF16), vm((2, 256, HEAD), BF16),
        vm((4, 2, 64, features), F32), vm((4, 64, features), BF16), vm((4, 64, features), BF16),
        vm((64, 256), BF16), vm((4, 64, 256), BF16), vm((4, 64, 256), BF16), vm((4, 64, 256), BF16),
        vm((2, 256, 256), BF16), vm((2, 256, 256), F32),
        vm((2, 256, HEAD), F32), vm((2, 256, HEAD), BF16), vm((2, 256, HEAD), F32),
        vm((2, 256, HEAD), BF16), vm((2, 256, 256), BF16),
        vm((8, 2, 256, 256), F32), vm((8, 2, 256, 256), F32), vm((8, 2, 64, 256), F32), vm((64, 256), F32),
    ]
    scratch += scatter_bufs(256) + scatter_bufs(256) + scatter_bufs(64)
    scratch += [dma(4), dma(4)] * 3
    scratch += [dma(4), dma(4), dma(4), dma(12), dma(1), dma(4)] * 3
    scratch += [dma(1), dma(4), dma(12), dma(12), dma(4), dma(4)] * 3
    scratch += [dma(10), dma(10), dma(3), dma(4), dma(3), dma(4), dma(2)]
    whole = pl.BlockSpec(memory_space=pltpu.VMEM)
    hbm = pl.BlockSpec(memory_space=pl.ANY)
    update, grad_text, grad_vision = pl.pallas_call(
        kernel,
        out_shape=(
            jax.ShapeDtypeStruct((256, 256), BF16),
            jax.ShapeDtypeStruct((256, 256), BF16),
            jax.ShapeDtypeStruct((features, 256), BF16),
        ),
        in_specs=[hbm, hbm, whole, whole, hbm, whole, whole, hbm],
        out_specs=(whole,) * 3,
        scratch_shapes=scratch,
        name="cross_attention",
        compiler_params=pltpu.CompilerParams(
            collective_id=0, has_side_effects=True, vmem_limit_bytes=60 * 2**20
        ),
    )(
        text, grad_out, vision.T, gate.reshape(1, 1),
        w_query, w_key, w_value, w_out,
    )
    return update, grad_text, grad_vision.T


def solution(mesh):
    return jax.shard_map(
        body,
        mesh=mesh,
        in_specs=(
            P("dp", "tensor"), P("dp", "tensor"), P("dp", "tensor"), P(),
            P("dp", "tensor"), P("tensor", "dp"), P("tensor", "dp"), P("tensor", "dp"),
        ),
        out_specs=(P("dp", "tensor"), P("dp", "tensor"), P("dp", "tensor")),
        check_vma=False,
    )
```

time: 161 us -> 131 us (0.81)
  Pallas kernels: 155 us -> 126 us
  local copies, waits for them, and re-layouts: 4.96 us -> 3.2 us
    pallas_call x1, Pallas kernels: 155 us -> 126 us  [body(): pl.pallas_call(kernel, out_shape=(jax.ShapeDtypeStruct((256, 256), BF16),...]
    unnamed x8 -> x7, local copies, waits for them, and re-layouts: 4.96 us -> 3.2 us
where the time goes in v2:
time: 131 us
  Pallas kernels  126 us (96%)
  local copies, waits for them, and re-layouts  3.2 us (2%)
    pallas_call x1, Pallas kernels, body(): pl.pallas_call(kernel, out_shape=(jax.ShapeDtypeStruct((256, 256), BF16),...  126 us
    unnamed x7, local copies, waits for them, and re-layouts  3.2 us

profile of v2, /device:TPU:1, one launch (start us, length us, event | category | flops | bytes accessed | tf_op | source)
XLA Modules:
  0.0 130.7 jit_solution(7181720776416086668)
XLA Ops:
  1.3 126.2 %cross_attention.1 = (bf16[256,256]{1,0:T(8,128)(2,1)}, bf16[256,256]{1,0:T(8,128)(2,1)}, bf16[240,256]{1,0:T(8,128)(2,1)}) custom-call(bf16[256,256]{1,0:T(8,128)(2,1)} %text.1, bf16[256,256]{1,0:T(8,128)(2,1)} %grad_out.1, bf16[240,256]{1,0:T(8,128)(2,1)} %bitcast.4, f32[1,1]{1,0:T(1,128)} %bitcast.3.gate, bf16[1024,256]{1,0:T(8,128)(2,1)} %w_query.1, ...), custom_call_target="tpu_custom_call" | custom-call | tf_op jit(solution)/shard_map/cross_attention/pallas_call | solution.py:661
  127.5 0.0 copy-start
  127.5 1.6 %copy.15 = bf16[256,256]{1,0:T(8,128)(2,1)} copy(bf16[256,256]{1,0:T(8,128)(2,1)} %get-tuple-element.12) | data formatting | bytes 262144
  129.1 0.0 copy-done
  129.1 0.0 copy-start.1
  129.1 0.7 copy.16
  129.7 0.3 copy-done.1
  130.0 0.6 copy.17
Async XLA Ops:
  127.5 1.6 %copy-start = (bf16[256,256]{1,0:T(8,128)(2,1)S(1)}, bf16[256,256]{1,0:T(8,128)(2,1)}, u32[]{:S(2)}) copy-start(bf16[256,256]{1,0:T(8,128)(2,1)} %get-tuple-element.13) | copy-start | bytes 393220
  129.1 0.9 copy-start.1

commit v3 on v2

--- a/solution.py
+++ b/solution.py
@@ -62,19 +62,15 @@
         copy.start()
         self.waits.append(copy.wait_send)
 
-    def start_unless_self(self, me, z, src, dst, send, recv, device):
-        @pl.when(z != me.z)
+    def start_if(self, cond, *args):
+        @pl.when(cond)
         def _():
-            rcopy(src, dst, send, recv, device).start()
-
-        @pl.when(z == me.z)
-        def _():
-            pltpu.make_async_copy(src, dst, recv).start()
+            rcopy(*args).start()
 
         def finish():
-            @pl.when(z != me.z)
+            @pl.when(cond)
             def _():
-                rcopy(src, dst, send, recv, device).wait_send()
+                rcopy(*args).wait_send()
 
         self.waits.append(finish)
 
@@ -119,7 +115,7 @@
         self.me, self.sends, self.own, self.buf = me, sends, own, buf
         self.zs, self.zr, self.ys, self.yr, self.cs, self.cr = sems
 
-    def start_z(self, later=False):
+    def start_z(self):
         me = self.me
         dst = self.buf.at[me.y, me.zh % 2, me.c, me.zl]
         recv = self.zr.at[(me.zh % 2) * 2 + me.zl]
@@ -127,22 +123,24 @@
         args = [
             (self.own, dst, self.zs.at[i], recv, me.at(z=(me.z + sign * one) % 8)) for i, sign in enumerate((1, -1))
         ]
-        self.sends.start(*args[0])
-        self.sends.waits.append(rcopy(*args[1]).wait_send)
-
-        def second():
-            rcopy(*args[1]).start()
+        for arg in args:
+            self.sends.start(*arg)
 
         @pl.when(me.kept)
         def _():
             pltpu.make_async_copy(self.own, dst, recv).start()
 
-        if not later:
-            second()
-            return None
-
-        pl.when(jnp.logical_not(me.kept))(second)
-        return lambda: pl.when(me.kept)(second)
+    def direct_z(self):
+        me = self.me
+        dst = self.buf.at[me.y, me.zh % 2, me.c, me.zl]
+        recv = self.zr.at[(me.zh % 2) * 2 + me.zl]
+        for i in range(4):
+            z = me.half + 2 * i
+            self.sends.start_if(z != me.z, self.own, dst, self.zs.at[i], recv, me.at(z=z))
+
+        @pl.when(me.kept)
+        def _():
+            pltpu.make_async_copy(self.own, dst, recv).start()
 
     def relay_z(self, i):
         if i == 3:
@@ -152,16 +150,7 @@
         block, sem = self.block(me.y, i), self.zs.at[2 + i % 2]
         args = block, block, sem, self.zr.at[me.order(i)], me.at(z=me.next_z)
 
-        @pl.when(cond)
-        def _():
-            rcopy(*args).start()
-
-        def finish():
-            @pl.when(cond)
-            def _():
-                rcopy(*args).wait_send()
-
-        self.sends.waits.append(finish)
+        self.sends.start_if(cond, *args)
 
     def block(self, slot, i):
         j = self.me.order(i)
@@ -171,10 +160,11 @@
         block = self.block(slot, i)
         rcopy(block, block, self.cs.at[0], self.cr.at[r], self.me.at(c=1 - self.me.c)).start()
 
-    def arrive(self, *positions):
+    def arrive(self, *positions, relay=True):
         for i in positions:
             arrived(self.block(self.me.y, i), self.zr.at[self.me.order(i)])
-            self.relay_z(i)
+            if relay:
+                self.relay_z(i)
 
     def start_y(self, *positions):
         me = self.me
@@ -219,7 +209,7 @@
 class Scatter:
     def __init__(self, me, sends, compute, acc, bufs, sems):
         self.me, self.sends, self.compute, self.acc = me, sends, compute, acc
-        self.pst, self.prv, self.fst, self.frv, self.nst, self.nrv, self.zst, self.zrv = bufs
+        self.pst, self.prv, self.fst, self.frv, self.nst, self.nrv, self.zst, self.zrv, self.tot = bufs
         self.cs, self.cr, self.ys, self.yr, self.zs, self.zr = sems
 
     def to_core(self, *rs):
@@ -250,25 +240,12 @@
         j = self.me.order(3 - i)
         return self.acc[r * 2 + j // 2, j % 2]
 
-    def send_far(self):
-        me = self.me
-        self.from_core(3)
-        for i in range(4):
+    def send_far(self, *positions):
+        for i in positions:
             self.fst[i] = self.mine(3, i).astype(BF16)
             self.sends.start(
-                self.fst.at[i], self.frv.at[i], self.ys.at[8 + i], self.yr.at[8 + i], me.at(dy=(1, -1)[i % 2])
+                self.fst.at[i], self.frv.at[i], self.ys.at[8 + i], self.yr.at[8 + i], self.me.at(dy=(1, -1)[i % 2])
             )
-
-    def begin(self):
-        self.to_core(3)
-        self.to_core(2, 1)
-        self.send_far()
-        self.from_core(2)
-        self.near((0, 1))
-        self.from_core(1)
-        self.near((1, 0))
-        self.to_core(0)
-        self.sends.waits.append(lambda: arrived(self.pst, self.cs.at[0]))
 
     def near(self, *items):
         me = self.me
@@ -281,7 +258,55 @@
             self.nst[s] = value.astype(BF16)
             self.sends.start(self.nst.at[s], self.nrv.at[s], self.ys.at[s], self.yr.at[s], me.at(dy=(1, -1)[way]))
 
+    def z_args(self, i):
+        me = self.me
+        place = me.place
+        j = me.order(3 - i)
+        if i < 3:
+            passes = (place != 1, place >= 2, place == 3)[i]
+            there = (jnp.where(place == 0, 1, place), 5 - place, 2)[i]
+            back = (place == 3) if i < 2 else False
+            via = (me.z + jnp.where(back, -2, 2) * (1 - 2 * me.zl)) % 8
+        else:
+            passes, there, via = False, 0, 0
+        second = jnp.where(me.zl == 0, 1, 2)
+        final = jnp.where(place == 1, jnp.where(j == second, 1, 0), jnp.where(place == 0, 0, 1))
+        slot = jnp.where(passes, 2 + there, final)
+        z = jnp.where(passes, via, 4 * me.zl + j)
+        return self.zst.at[i], self.zrv.at[slot], self.zs.at[i], self.zr.at[slot], me.at(z=z)
+
     def start_z(self, *positions):
+        me = self.me
+        place = me.place
+        for i in positions:
+            total = self.mine(0, i)
+            for way in range(2):
+                s = way * 4 + i
+                arrived(self.nrv.at[s], self.yr.at[s])
+                total = total + self.nrv[s].astype(F32)
+            adds = (None, place == 1, place != 1, place >= 2)[i]
+            if adds is None:
+                self.zst[i] = total.astype(BF16)
+            else:
+                self.tot[i // 3] = total
+
+                @pl.when(adds)
+                def _():
+                    arrived(self.zrv.at[2 + i], self.zr.at[2 + i])
+                    self.tot[i // 3] += self.zrv[2 + i].astype(F32)
+
+                self.zst[i] = self.tot[i // 3].astype(BF16)
+            if i < 3:
+                rcopy(*self.z_args(i)).start()
+            else:
+                pl.when(jnp.logical_not(me.kept))(lambda: rcopy(*self.z_args(3)).start())
+
+    def sent_z(self):
+        for i in range(3):
+            rcopy(*self.z_args(i)).wait_send()
+        pl.when(jnp.logical_not(self.me.kept))(lambda: rcopy(*self.z_args(3)).wait_send())
+
+    def direct_z(self, *positions):
         me = self.me
         for i in positions:
             total = self.mine(0, i)
@@ -291,15 +316,55 @@
                 total = total + self.nrv[s].astype(F32)
             self.zst[i] = total.astype(BF16)
             z = 4 * me.zl + me.order(3 - i)
-            self.sends.start_unless_self(
-                me, z, self.zst.at[i], self.zrv.at[me.zh], self.zs.at[i], self.zr.at[me.zh], me.at(z=z)
-            )
+            there, recv = self.zrv.at[me.zh], self.zr.at[me.zh]
+            args = self.zst.at[i], there, self.zs.at[i], recv, me.at(z=z)
+            if i < 3:
+                self.sends.start(*args)
+            else:
+                self.sends.start_if(jnp.logical_not(me.kept), *args)
+
+                @pl.when(me.kept)
+                def _():
+                    pltpu.make_async_copy(self.zst.at[3], there, recv).start()
 
     def total(self):
+        value = jnp.where(self.me.kept, self.tot[1], 0.0)
+        for s in range(2):
+            arrived(self.zrv.at[s], self.zr.at[s])
+            value = value + self.zrv[s].astype(F32)
+        return value
+
+    def direct_total(self):
         value = None
         for s in range(4):
             arrived(self.zrv.at[s], self.zr.at[s])
             term = self.zrv[s].astype(F32)
+            value = term if value is None else value + term
+        return value
+
+    def both_z(self, *positions):
+        me = self.me
+        for i in positions:
+            total = self.mine(0, i)
+            for way in range(2):
+                s = way * 4 + i
+                arrived(self.nrv.at[s], self.yr.at[s])
+                total = total + self.nrv[s].astype(F32)
+            self.zst[i] = total.astype(BF16)
+            j = me.order(3 - i)
+            there = (j // 2) * 4 + me.zh
+            for k in range(2):
+                z = 4 * me.zl + 2 * k + j % 2
+                args = self.zst.at[i], self.zrv.at[there], self.zs.at[i * 2 + k], self.zr.at[there], me.at(z=z)
+                self.sends.start_if(z != me.z, *args)
+                local = pltpu.make_async_copy(*args[:2], args[3])
+                pl.when(z == me.z)(local.start)
+
+    def both_total(self, k):
+        value = None
+        for s in range(4):
+            arrived(self.zrv.at[k * 4 + s], self.zr.at[k * 4 + s])
+            term = self.zrv[k * 4 + s].astype(F32)
             value = term if value is None else value + term
         return value
 
@@ -311,8 +376,8 @@
     probs_low, probs, query, query_low, query_scale, attend_grad, score_grad, acc_o, acc_t, acc_v, own_kv,
     *rest,
 ):
-    o_bufs, t_bufs, v_bufs = rest[0:8], rest[8:16], rest[16:24]
-    rest = rest[24:]
+    o_bufs, t_bufs, v_bufs = rest[0:9], rest[9:18], rest[18:27]
+    rest = rest[27:]
     x_sems = [rest[2 * i : 2 * i + 2] for i in range(3)]
     rest = rest[6:]
     g_sems = [rest[6 * i : 6 * i + 6] for i in range(3)]
@@ -365,7 +430,7 @@
     wkv_g[me.x, :, HEAD:] = w_value[...]
     pl.semaphore_wait(barrier, jnp.where(me.kept, 14, 17))
 
-    second = g_text.start_z(later=True)
+    g_text.start_z()
     gx_kv.start()
     exchange(0, vision, vis_g)
 
@@ -381,7 +446,6 @@
     gx_kv.relay(0)
     gx_kv.relay(1)
     gx_q.start()
-    second()
 
     @pl.when(jnp.logical_not(me.kept))
     def _():
@@ -400,27 +464,30 @@
     gx_kv.finish()
     s_kv = Scatter(me, sends, kv_block, acc_v, v_bufs, r_sems[2])
     s_kv.to_core(3, 2, 1, 0)
+    sends.waits.append(lambda: arrived(s_kv.pst, s_kv.cs.at[0]))
+    g_text.near(1)
     g_text.arrive(3)
     g_text.start_y(3)
     g_grad.start_z()
-    s_kv.send_far()
-    g_text.near(1)
+    s_kv.from_core(3)
+    s_kv.send_far(0, 1, 2, 3)
     s_kv.from_core(2)
     s_kv.from_core(1)
     s_kv.near((0, 1), (1, 0), (0, 3), (1, 2))
     s_kv.from_core(0)
-    sends.waits.append(lambda: arrived(s_kv.pst, s_kv.cs.at[0]))
     g_text.near(2)
     gx_q.relay(0)
     gx_q.relay(1)
     gx_o.start()
     s_kv.near((0, 0), (1, 1), (0, 2), (1, 3))
+    g_text.near(3)
     g_grad.arrive(0)
-    g_text.near(3)
+    g_grad.start_y(0)
+    s_kv.both_z(0, 1, 2, 3)
     g_grad.arrive(1)
-    g_grad.start_y(0, 1)
-    s_kv.start_z(0, 1, 2, 3)
-
+    g_grad.start_y(1)
+    g_text.far(0, 1, 2, 3)
+    g_text.from_core(0, 1, 2)
     def q_part(slot):
         total = None
         for j in range(4):
@@ -428,16 +495,14 @@
             total = term if total is None else total + term
         return total.reshape(2, 256, 256)
 
-    g_text.far(0, 1, 2, 3)
-    g_grad.arrive(2)
-    g_grad.start_y(2)
-    g_text.from_core(0, 1, 2)
     local_q.wait()
     gx_q.finish()
     with jax.named_scope("query"):
         q_acc[...] = q_part(near_y[0])
         q_acc[...] += q_part(near_y[1])
         q_acc[...] += q_part(near_y[2])
+    g_grad.arrive(2)
+    g_grad.start_y(2)
     g_text.from_core(3)
     with jax.named_scope("query_last"):
         q_acc[...] += q_part(near_y[3])
@@ -446,23 +511,26 @@
             exchange(1 + h, q_st.at[h], q_rv.at[h])
     g_grad.arrive(3)
     g_grad.start_y(3)
-
+    g_grad.near(0)
+    gx_o.relay(0)
+    gx_o.relay(1)
     with jax.named_scope("kv"):
-        projected = s_kv.total()
-        keys = projected[:, :HEAD]
-        key_scale = lax.rsqrt(jnp.mean(keys * keys, axis=-1, keepdims=True) + EPS)
-        kv_all[piece, :, :HEAD] = (keys * key_scale).astype(BF16)
-        kv_all[piece, :, HEAD:] = projected[:, HEAD:].astype(BF16)
-        own_kv[...] = projected
-        for j in range(3):
-            p, device = mate(j)
-            sends.start(kv_all.at[piece], kv_all.at[piece], m_ss.at[j], m_rs.at[piece], device)
-
-    g_grad.near(0)
+        rows = []
+        for k in range(2):
+            projected = s_kv.both_total(k)
+            rows.append(projected)
+            keys = projected[:, :HEAD]
+            key_scale = lax.rsqrt(jnp.mean(keys * keys, axis=-1, keepdims=True) + EPS)
+            p = k * 2 + me.c
+            kv_all[p, :, :HEAD] = (keys * key_scale).astype(BF16)
+            kv_all[p, :, HEAD:] = projected[:, HEAD:].astype(BF16)
+            sends.start(kv_all.at[p], kv_all.at[p], m_ss.at[k], m_rs.at[k], me.at(c=1 - me.c))
+        own_kv[...] = jnp.where(me.zh % 2 == 0, rows[0], rows[1])
+
+    g_grad.near(1)
     with jax.named_scope("kv_wait"):
-        for j in range(3):
-            p, _ = mate(j)
-            arrived(kv_all.at[p], m_rs.at[p])
+        for k in range(2):
+            arrived(kv_all.at[k * 2 + 1 - me.c], m_rs.at[k])
     kv = kv_all[...].reshape(256, 256)
     key_head, value_head = kv[:, :HEAD], kv[:, HEAD:]
     scale = HEAD ** (-0.5)
@@ -486,10 +554,7 @@
             probs_low[h] = low
             att_g[me.zl, :, own] = dot(low, value_head).astype(BF16)
             exchange(3 + h, att_g.at[me.zl, :, own], att_g.at[me.zl, :, own])
-    g_grad.near(1, 2)
-    gx_o.relay(0)
-    gx_o.relay(1)
-    g_grad.near(3)
+        g_grad.near(2 + h)
 
     def ag_part(slot):
         total = None
@@ -498,6 +563,9 @@
             total = term if total is None else total + term
         return total.reshape(2, 256, 256)
 
+    local_o.wait()
+    gx_o.finish()
+
     def out_block(slot, k, cc):
         block = wo_g[slot, :, pl.ds(pl.multiple_of((k * 2 + cc) * 256, 256), 256)]
         return dot(att_g[...].reshape(512, 256), block)
@@ -507,26 +575,32 @@
             theirs = att_g.at[1 - me.zl, :, pl.ds(h * HEAD, HEAD)]
             arrived(theirs, e_rs.at[3 + h])
     s_out = Scatter(me, sends, out_block, acc_o, o_bufs, r_sems[0])
-    g_grad.far(0, 1)
-    local_o.wait()
-    gx_o.finish()
-    s_out.begin()
-    s_out.near((0, 3), (1, 2))
-
-    g_grad.far(2, 3)
+    s_out.to_core(3)
+    s_out.to_core(2)
+    s_out.from_core(3)
+    s_out.send_far(0, 1)
+    s_out.to_core(1)
+    s_out.from_core(2)
+    s_out.near((0, 1))
+    s_out.from_core(1)
+    s_out.near((1, 0))
+    s_out.send_far(2, 3)
     g_grad.from_core(0, 1, 2)
     with jax.named_scope("attend_grad"):
         ag_acc[...] = ag_part(near_y[0])
         ag_acc[...] += ag_part(near_y[1])
         ag_acc[...] += ag_part(near_y[2])
+    g_grad.far(0, 1, 2, 3)
     g_grad.from_core(3)
     with jax.named_scope("attend_grad_last"):
         ag_acc[...] += ag_part(near_y[3])
         for h in range(2):
             ag_st[h] = ag_acc[1 - me.zl, :, h * HEAD : (h + 1) * HEAD].astype(BF16)
             exchange(5 + h, ag_st.at[h], ag_rv.at[h])
+    s_out.near((0, 0), (1, 1), (0, 3), (1, 2))
+    s_out.to_core(0)
+    sends.waits.append(lambda: arrived(s_out.pst, s_out.cs.at[0]))
     s_out.from_core(0)
-    s_out.near((0, 0), (1, 1))
 
     for h in range(2):
         own = slice(h * HEAD, (h + 1) * HEAD)
@@ -545,8 +619,8 @@
             mean = jnp.mean(normed_grad * q, axis=-1, keepdims=True)
             q_grad = q_scale * (normed_grad - q * (q_scale * q_scale) * mean)
             dq_g[me.zl, :, own] = q_grad.astype(BF16)
+        exchange(7 + h, dq_g.at[me.zl, :, own], dq_g.at[me.zl, :, own])
         if h == 0:
-            exchange(7, dq_g.at[me.zl, :, own], dq_g.at[me.zl, :, own])
             s_out.near((0, 2), (1, 3))
     with jax.named_scope("kv_part"):
         key_part = dot(score_grad[0], query_low[0], TN) + dot(score_grad[1], query_low[1], TN)
@@ -556,7 +630,20 @@
         for j in range(3):
             p, device = mate(j)
             sends.start(kvp.at[p], kvp_rv.at[piece], n_ss.at[j], n_rs.at[piece], device)
-    exchange(8, dq_g.at[me.zl, :, HEAD:], dq_g.at[me.zl, :, HEAD:])
+
+    def text_block(slot, k, cc):
+        block = wq_g[slot, pl.ds(pl.multiple_of((k * 2 + cc) * 256, 256), 256), :]
+        return dot(dq_g[...].reshape(512, 256), block, NT)
+
+    with jax.named_scope("dq_wait"):
+        for h in range(2):
+            theirs = dq_g.at[1 - me.zl, :, pl.ds(h * HEAD, HEAD)]
+            arrived(theirs, e_rs.at[7 + h])
+    s_text = Scatter(me, sends, text_block, acc_t, t_bufs, r_sems[1])
+    s_text.to_core(3)
+    s_text.to_core(2)
+    s_text.from_core(3)
+    s_text.send_far(0, 1)
 
     with jax.named_scope("kv_grad"):
         kv_grad = kvp[piece].astype(F32)
@@ -571,35 +658,28 @@
         k_grad = key_scale * k_grad - keys * (key_scale * key_scale * key_scale) * mean
         jg[:, :HEAD] = k_grad.astype(BF16)
         jg[:, HEAD:] = kv_grad[:, HEAD:].astype(BF16)
-        g_kv.start_z()
-
-    def text_block(slot, k, cc):
-        block = wq_g[slot, pl.ds(pl.multiple_of((k * 2 + cc) * 256, 256), 256), :]
-        return dot(dq_g[...].reshape(512, 256), block, NT)
-
-    with jax.named_scope("dq_wait"):
-        for h in range(2):
-            theirs = dq_g.at[1 - me.zl, :, pl.ds(h * HEAD, HEAD)]
-            arrived(theirs, e_rs.at[7 + h])
-    s_text = Scatter(me, sends, text_block, acc_t, t_bufs, r_sems[1])
-    s_text.to_core(3)
-    s_text.to_core(2, 1)
-    s_text.send_far()
-    g_kv.arrive(0, 1)
+        g_kv.direct_z()
+
+    s_text.to_core(1)
+    s_out.direct_z(0, 1)
     s_text.from_core(2)
     s_text.near((0, 1))
     s_text.from_core(1)
     s_text.near((1, 0))
+
+    s_text.near((0, 0), (1, 1))
+    s_text.send_far(2, 3)
+    s_out.direct_z(2, 3)
     s_text.to_core(0)
     sends.waits.append(lambda: arrived(s_text.pst, s_text.cs.at[0]))
-    g_kv.arrive(2, 3)
+    s_text.from_core(0)
+    g_kv.arrive(0, 1, 2, 3, relay=False)
     g_kv.start_y(0, 1, 2, 3)
-    s_text.from_core(0)
-    s_out.start_z(0, 1, 2, 3)
-    s_text.near((0, 0), (1, 1))
+    s_text.near((0, 3), (1, 2))
+    s_text.direct_z(0, 1)
+    s_text.near((0, 2), (1, 3))
     g_kv.near(0, 1, 2, 3)
-    s_text.near((0, 2), (1, 2), (0, 3), (1, 3))
-    s_text.start_z(0)
+    s_text.direct_z(2, 3)
     g_kv.far(0, 1, 2, 3)
     g_kv.from_core(0, 1, 2, 3)
 
@@ -611,17 +691,21 @@
         gv_acc[...] = gv.reshape(4, 2, 64, -1)
         gv_st[...] = gv_acc[:, 1 - me.zl].astype(BF16)
         exchange(9, gv_st, gv_rv)
-    s_text.start_z(1, 2, 3)
+    with jax.named_scope("update"):
+        update[...] = (tanh_gate * s_out.direct_total()).astype(BF16)
     with jax.named_scope("vision_grad_last"):
         arrived(gv_rv, e_rs.at[9])
         total = gv_acc[:, me.zl] + gv_rv[...].astype(F32)
         grad_vision[...] = total.reshape(256, -1).T.astype(BF16)
-    with jax.named_scope("update"):
-        update[...] = (tanh_gate * s_out.total()).astype(BF16)
     with jax.named_scope("text_grad_last"):
-        grad_text[...] = s_text.total().astype(BF16)
+        grad_text[...] = s_text.direct_total().astype(BF16)
     with jax.named_scope("sends"):
         sends.finish()
+
+
+def hand_on(*refs):
+    for n in range(3):
+        refs[3 + n][...] = refs[n][...]
 
 
 def body(text, grad_out, vision, gate, w_query, w_key, w_value, w_out):
@@ -634,7 +718,7 @@
             vm((8, 2 * m, 256), BF16), vm((8, 2 * m, 256), BF16),
             vm((4, m, 256), BF16), vm((4, m, 256), BF16),
             vm((8, m, 256), BF16), vm((8, m, 256), BF16),
-            vm((4, m, 256), BF16), vm((4, m, 256), BF16),
+            vm((4, m, 256), BF16), vm((8 if m == 64 else 6, m, 256), BF16), vm((2, m, 256), F32),
         ]
 
     scratch = [
@@ -654,8 +738,8 @@
     scratch += scatter_bufs(256) + scatter_bufs(256) + scatter_bufs(64)
     scratch += [dma(4), dma(4)] * 3
     scratch += [dma(4), dma(4), dma(4), dma(12), dma(1), dma(4)] * 3
-    scratch += [dma(1), dma(4), dma(12), dma(12), dma(4), dma(4)] * 3
-    scratch += [dma(10), dma(10), dma(3), dma(4), dma(3), dma(4), dma(2)]
+    scratch += [dma(1), dma(4), dma(12), dma(12), dma(8), dma(8)] * 3
+    scratch += [dma(10), dma(10), dma(2), dma(2), dma(3), dma(4), dma(2)]
     whole = pl.BlockSpec(memory_space=pltpu.VMEM)
     hbm = pl.BlockSpec(memory_space=pl.ANY)
     update, grad_text, grad_vision = pl.pallas_call(
@@ -676,6 +760,13 @@
         text, grad_out, vision.T, gate.reshape(1, 1),
         w_query, w_key, w_value, w_out,
     )
+    update, grad_text, grad_vision = pl.pallas_call(
+        hand_on,
+        out_shape=(update, grad_text, grad_vision),
+        in_specs=[whole] * 3,
+        out_specs=(whole,) * 3,
+        name="hand_on",
+    )(update, grad_text, grad_vision)
     return update, grad_text, grad_vision.T
 
 

time: 131 us -> 122 us (0.931)
  Pallas kernels: 126 us -> 120 us
  local copies, waits for them, and re-layouts: 3.2 us -> 0 us
    pallas_call x1, Pallas kernels: 126 us -> 118 us  [body(): pl.pallas_call(kernel, out_shape=(jax.ShapeDtypeStruct((256, 256), BF16),...]
    unnamed x7 -> x0, local copies, waits for them, and re-layouts: 3.2 us -> none
    pallas_call x0 -> x1, Pallas kernels: none -> 1.77 us  [body(): pl.pallas_call(hand_on, out_shape=(update, grad_text, grad_vision), in_sp...]
where the time goes in v3:
time: 122 us
  Pallas kernels  120 us (98%)
  between operations  1.29 us (1%)
    pallas_call x1, Pallas kernels, body(): pl.pallas_call(kernel, out_shape=(jax.ShapeDtypeStruct((256, 256), BF16),...  118 us

profile of v3, /device:TPU:1, one launch (start us, length us, event | category | flops | bytes accessed | tf_op | source)
XLA Modules:
  0.0 121.5 jit_solution(15257500934034284739)
XLA Ops:
  1.3 118.5 %cross_attention.1 = (bf16[256,256]{1,0:T(8,128)(2,1)}, bf16[256,256]{1,0:T(8,128)(2,1)}, bf16[240,256]{1,0:T(8,128)(2,1)}) custom-call(bf16[256,256]{1,0:T(8,128)(2,1)} %text.1, bf16[256,256]{1,0:T(8,128)(2,1)} %grad_out.1, bf16[240,256]{1,0:T(8,128)(2,1)} %bitcast.4, f32[1,1]{1,0:T(1,128)} %bitcast.3.gate, bf16[1024,256]{1,0:T(8,128)(2,1)} %w_query.1, ...), custom_call_target="tpu_custom_call" | custom-call | tf_op jit(solution)/shard_map/cross_attention/pallas_call | solution.py:745
  119.7 1.8 %hand_on.1 = (bf16[256,256]{1,0:T(8,128)(2,1)}, bf16[256,256]{1,0:T(8,128)(2,1)}, bf16[240,256]{1,0:T(8,128)(2,1)}) custom-call(bf16[256,256]{1,0:T(8,128)(2,1)} %get-tuple-element.9.refs_0_, bf16[256,256]{1,0:T(8,128)(2,1)} %get-tuple-element.10.refs_1_, bf16[240,256]{1,0:T(8,128)(2,1)} %get-tuple-element.11.refs_2_), custom_call_target="tpu_custom_call" | custom-call | tf_op jit(solution)/shard_map/hand_on/pallas_call | solution.py:763

commit v4 on v3

--- a/solution.py
+++ b/solution.py
@@ -209,7 +209,7 @@
 class Scatter:
     def __init__(self, me, sends, compute, acc, bufs, sems):
         self.me, self.sends, self.compute, self.acc = me, sends, compute, acc
-        self.pst, self.prv, self.fst, self.frv, self.nst, self.nrv, self.zst, self.zrv, self.tot = bufs
+        self.pst, self.prv, self.fst, self.frv, self.nst, self.nrv, self.zst, self.zrv = bufs
         self.cs, self.cr, self.ys, self.yr, self.zs, self.zr = sems
 
     def to_core(self, *rs):
@@ -260,53 +260,15 @@
 
     def z_args(self, i):
         me = self.me
-        place = me.place
-        j = me.order(3 - i)
-        if i < 3:
-            passes = (place != 1, place >= 2, place == 3)[i]
-            there = (jnp.where(place == 0, 1, place), 5 - place, 2)[i]
-            back = (place == 3) if i < 2 else False
-            via = (me.z + jnp.where(back, -2, 2) * (1 - 2 * me.zl)) % 8
-        else:
-            passes, there, via = False, 0, 0
-        second = jnp.where(me.zl == 0, 1, 2)
-        final = jnp.where(place == 1, jnp.where(j == second, 1, 0), jnp.where(place == 0, 0, 1))
-        slot = jnp.where(passes, 2 + there, final)
-        z = jnp.where(passes, via, 4 * me.zl + j)
+        slot = jnp.minimum(me.place, 2)
+        z = 4 * me.zl + me.order(3 - i)
+        if i < 2:
+            passes = me.place >= 2
+            slot = jnp.where(passes, 1 + (me.place, 5 - me.place)[i], slot)
+            z = jnp.where(passes, me.next_z, z)
         return self.zst.at[i], self.zrv.at[slot], self.zs.at[i], self.zr.at[slot], me.at(z=z)
 
     def start_z(self, *positions):
-        me = self.me
-        place = me.place
-        for i in positions:
-            total = self.mine(0, i)
-            for way in range(2):
-                s = way * 4 + i
-                arrived(self.nrv.at[s], self.yr.at[s])
-                total = total + self.nrv[s].astype(F32)
-            adds = (None, place == 1, place != 1, place >= 2)[i]
-            if adds is None:
-                self.zst[i] = total.astype(BF16)
-            else:
-                self.tot[i // 3] = total
-
-                @pl.when(adds)
-                def _():
-                    arrived(self.zrv.at[2 + i], self.zr.at[2 + i])
-                    self.tot[i // 3] += self.zrv[2 + i].astype(F32)
-
-                self.zst[i] = self.tot[i // 3].astype(BF16)
-            if i < 3:
-                rcopy(*self.z_args(i)).start()
-            else:
-                pl.when(jnp.logical_not(me.kept))(lambda: rcopy(*self.z_args(3)).start())
-
-    def sent_z(self):
-        for i in range(3):
-            rcopy(*self.z_args(i)).wait_send()
-        pl.when(jnp.logical_not(self.me.kept))(lambda: rcopy(*self.z_args(3)).wait_send())
-
-    def direct_z(self, *positions):
         me = self.me
         for i in positions:
             total = self.mine(0, i)
@@ -315,9 +277,14 @@
                 arrived(self.nrv.at[s], self.yr.at[s])
                 total = total + self.nrv[s].astype(F32)
             self.zst[i] = total.astype(BF16)
-            z = 4 * me.zl + me.order(3 - i)
-            there, recv = self.zrv.at[me.zh], self.zr.at[me.zh]
-            args = self.zst.at[i], there, self.zs.at[i], recv, me.at(z=z)
+            if i >= 2:
+
+                @pl.when(me.place >= 2)
+                def _():
+                    arrived(self.zrv.at[1 + i], self.zr.at[1 + i])
+                    self.zst[i] = (total + self.zrv[1 + i].astype(F32)).astype(BF16)
+
+            args = self.z_args(i)
             if i < 3:
                 self.sends.start(*args)
             else:
@@ -325,18 +292,11 @@
 
                 @pl.when(me.kept)
                 def _():
-                    pltpu.make_async_copy(self.zst.at[3], there, recv).start()
+                    pltpu.make_async_copy(args[0], args[1], args[3]).start()
 
     def total(self):
-        value = jnp.where(self.me.kept, self.tot[1], 0.0)
-        for s in range(2):
-            arrived(self.zrv.at[s], self.zr.at[s])
-            value = value + self.zrv[s].astype(F32)
-        return value
-
-    def direct_total(self):
         value = None
-        for s in range(4):
+        for s in range(3):
             arrived(self.zrv.at[s], self.zr.at[s])
             term = self.zrv[s].astype(F32)
             value = term if value is None else value + term
@@ -376,8 +336,8 @@
     probs_low, probs, query, query_low, query_scale, attend_grad, score_grad, acc_o, acc_t, acc_v, own_kv,
     *rest,
 ):
-    o_bufs, t_bufs, v_bufs = rest[0:9], rest[9:18], rest[18:27]
-    rest = rest[27:]
+    o_bufs, t_bufs, v_bufs = rest[0:8], rest[8:16], rest[16:24]
+    rest = rest[24:]
     x_sems = [rest[2 * i : 2 * i + 2] for i in range(3)]
     rest = rest[6:]
     g_sems = [rest[6 * i : 6 * i + 6] for i in range(3)]
@@ -631,6 +591,8 @@
             p, device = mate(j)
             sends.start(kvp.at[p], kvp_rv.at[piece], n_ss.at[j], n_rs.at[piece], device)
 
+    s_out.start_z(0, 1)
+
     def text_block(slot, k, cc):
         block = wq_g[slot, pl.ds(pl.multiple_of((k * 2 + cc) * 256, 256), 256), :]
         return dot(dq_g[...].reshape(512, 256), block, NT)
@@ -644,6 +606,16 @@
     s_text.to_core(2)
     s_text.from_core(3)
     s_text.send_far(0, 1)
+
+    s_text.to_core(1)
+    s_text.from_core(2)
+    s_text.near((0, 1))
+    s_text.from_core(1)
+    s_text.near((1, 0), (0, 0), (1, 1))
+    s_text.send_far(2, 3)
+    s_text.near((0, 3), (1, 2))
+    s_text.to_core(0)
+    sends.waits.append(lambda: arrived(s_text.pst, s_text.cs.at[0]))
 
     with jax.named_scope("kv_grad"):
         kv_grad = kvp[piece].astype(F32)
@@ -660,26 +632,14 @@
         jg[:, HEAD:] = kv_grad[:, HEAD:].astype(BF16)
         g_kv.direct_z()
 
-    s_text.to_core(1)
-    s_out.direct_z(0, 1)
-    s_text.from_core(2)
-    s_text.near((0, 1))
-    s_text.from_core(1)
-    s_text.near((1, 0))
-
-    s_text.near((0, 0), (1, 1))
-    s_text.send_far(2, 3)
-    s_out.direct_z(2, 3)
-    s_text.to_core(0)
-    sends.waits.append(lambda: arrived(s_text.pst, s_text.cs.at[0]))
+    s_out.start_z(2, 3)
     s_text.from_core(0)
+    s_text.start_z(0, 1)
+    s_text.near((0, 2), (1, 3))
     g_kv.arrive(0, 1, 2, 3, relay=False)
     g_kv.start_y(0, 1, 2, 3)
-    s_text.near((0, 3), (1, 2))
-    s_text.direct_z(0, 1)
-    s_text.near((0, 2), (1, 3))
     g_kv.near(0, 1, 2, 3)
-    s_text.direct_z(2, 3)
+    s_text.start_z(2, 3)
     g_kv.far(0, 1, 2, 3)
     g_kv.from_core(0, 1, 2, 3)
 
@@ -692,13 +652,13 @@
         gv_st[...] = gv_acc[:, 1 - me.zl].astype(BF16)
         exchange(9, gv_st, gv_rv)
     with jax.named_scope("update"):
-        update[...] = (tanh_gate * s_out.direct_total()).astype(BF16)
+        update[...] = (tanh_gate * s_out.total()).astype(BF16)
     with jax.named_scope("vision_grad_last"):
         arrived(gv_rv, e_rs.at[9])
         total = gv_acc[:, me.zl] + gv_rv[...].astype(F32)
         grad_vision[...] = total.reshape(256, -1).T.astype(BF16)
     with jax.named_scope("text_grad_last"):
-        grad_text[...] = s_text.direct_total().astype(BF16)
+        grad_text[...] = s_text.total().astype(BF16)
     with jax.named_scope("sends"):
         sends.finish()
 
@@ -718,7 +678,7 @@
             vm((8, 2 * m, 256), BF16), vm((8, 2 * m, 256), BF16),
             vm((4, m, 256), BF16), vm((4, m, 256), BF16),
             vm((8, m, 256), BF16), vm((8, m, 256), BF16),
-            vm((4, m, 256), BF16), vm((8 if m == 64 else 6, m, 256), BF16), vm((2, m, 256), F32),
+            vm((4, m, 256), BF16), vm((8 if m == 64 else 5, m, 256), BF16),
         ]
 
     scratch = [

time: 122 us -> 119 us (0.975)
  Pallas kernels: 120 us -> 117 us
    pallas_call x1, Pallas kernels: 118 us -> 115 us  [body(): pl.pallas_call(kernel, out_shape=(jax.ShapeDtypeStruct((256, 256), BF16),...]
where the time goes in v4:
time: 119 us; the launch traced here: 118 us
  Pallas kernels  117 us (98%)
  between operations  1.29 us (1%)
    pallas_call x1, Pallas kernels, body(): pl.pallas_call(kernel, out_shape=(jax.ShapeDtypeStruct((256, 256), BF16),...  115 us

profile of v4, /device:TPU:1, one launch (start us, length us, event | category | flops | bytes accessed | tf_op | source)
XLA Modules:
  0.0 118.4 jit_solution(16102418754990981027)
XLA Ops:
  1.3 115.3 %cross_attention.1 = (bf16[256,256]{1,0:T(8,128)(2,1)}, bf16[256,256]{1,0:T(8,128)(2,1)}, bf16[240,256]{1,0:T(8,128)(2,1)}) custom-call(bf16[256,256]{1,0:T(8,128)(2,1)} %text.1, bf16[256,256]{1,0:T(8,128)(2,1)} %grad_out.1, bf16[240,256]{1,0:T(8,128)(2,1)} %bitcast.4, f32[1,1]{1,0:T(1,128)} %bitcast.3.gate, bf16[1024,256]{1,0:T(8,128)(2,1)} %w_query.1, ...), custom_call_target="tpu_custom_call" | custom-call | tf_op jit(solution)/shard_map/cross_attention/pallas_call | solution.py:705
  116.6 1.8 %hand_on.1 = (bf16[256,256]{1,0:T(8,128)(2,1)}, bf16[256,256]{1,0:T(8,128)(2,1)}, bf16[240,256]{1,0:T(8,128)(2,1)}) custom-call(bf16[256,256]{1,0:T(8,128)(2,1)} %get-tuple-element.9.refs_0_, bf16[256,256]{1,0:T(8,128)(2,1)} %get-tuple-element.10.refs_1_, bf16[240,256]{1,0:T(8,128)(2,1)} %get-tuple-element.11.refs_2_), custom_call_target="tpu_custom_call" | custom-call | tf_op jit(solution)/shard_map/hand_on/pallas_call | solution.py:723

commit v5 on v4

--- a/solution.py
+++ b/solution.py
@@ -444,9 +444,9 @@
     g_grad.arrive(0)
     g_grad.start_y(0)
     s_kv.both_z(0, 1, 2, 3)
+    g_text.far(0, 1, 2, 3)
     g_grad.arrive(1)
     g_grad.start_y(1)
-    g_text.far(0, 1, 2, 3)
     g_text.from_core(0, 1, 2)
     def q_part(slot):
         total = None

time: 119 us -> 125 us (1.050)
  Pallas kernels: 117 us -> 123 us
    pallas_call x1, Pallas kernels: 115 us -> 122 us  [body(): pl.pallas_call(kernel, out_shape=(jax.ShapeDtypeStruct((256, 256), BF16),...]
where the time goes in v5:
time: 125 us
  Pallas kernels  123 us (98%)
  between operations  1.29 us (1%)
    pallas_call x1, Pallas kernels, body(): pl.pallas_call(kernel, out_shape=(jax.ShapeDtypeStruct((256, 256), BF16),...  122 us

profile of v5, /device:TPU:1, one launch (start us, length us, event | category | flops | bytes accessed | tf_op | source)
XLA Modules:
  0.0 124.7 jit_solution(18168784044752953448)
XLA Ops:
  1.3 121.6 %cross_attention.1 = (bf16[256,256]{1,0:T(8,128)(2,1)}, bf16[256,256]{1,0:T(8,128)(2,1)}, bf16[240,256]{1,0:T(8,128)(2,1)}) custom-call(bf16[256,256]{1,0:T(8,128)(2,1)} %text.1, bf16[256,256]{1,0:T(8,128)(2,1)} %grad_out.1, bf16[240,256]{1,0:T(8,128)(2,1)} %bitcast.4, f32[1,1]{1,0:T(1,128)} %bitcast.3.gate, bf16[1024,256]{1,0:T(8,128)(2,1)} %w_query.1, ...), custom_call_target="tpu_custom_call" | custom-call | tf_op jit(solution)/shard_map/cross_attention/pallas_call | solution.py:705
  122.9 1.8 %hand_on.1 = (bf16[256,256]{1,0:T(8,128)(2,1)}, bf16[256,256]{1,0:T(8,128)(2,1)}, bf16[240,256]{1,0:T(8,128)(2,1)}) custom-call(bf16[256,256]{1,0:T(8,128)(2,1)} %get-tuple-element.9.refs_0_, bf16[256,256]{1,0:T(8,128)(2,1)} %get-tuple-element.10.refs_1_, bf16[240,256]{1,0:T(8,128)(2,1)} %get-tuple-element.11.refs_2_), custom_call_target="tpu_custom_call" | custom-call | tf_op jit(solution)/shard_map/hand_on/pallas_call | solution.py:723
